TPU v7x, 32 devices: a whole 2x2x4 slice. The times are simulated.
32 devices in a mesh: aux: 16 (over z, y, x), bas: 2 (over core).
Axes of the slice: x: 2, y: 2, z: 4, core: 2. Of those that a mesh axis runs over, the one named last changes fastest.
Arguments:
- integrals: bfloat16 [16, 32, 3, 128, 128], P('aux', 'bas'), may hold values from -0.125 to 0.125
- orbitals: bfloat16 [32, 128, 128], P('bas'), may hold values from -0.5 to 0.5
- locality: int32 [32], P('bas'), may hold values from 0 to 15, as said below
- screen: int32 [16, 32, 3], P('aux', 'bas'), may hold values 0 or 1
- metric: bfloat16 [16, 16], replicated, may hold values from -1 to 3
Outputs:
- exchange_band: float32 [32, 5, 16384], P('bas', None, 'aux')
Inputs may be any that keep to these rules, and one draw needn't show every extreme that they name: `locality`: within each bas shard, its 16 orbital tiles name each of its 16 blocks exactly once.
All inputs are finite; a program needn't handle non-finite values. No bound on the sum of `screen` on one device may be relied on, other than what follows from the above.
Results may differ from a plain program's by a relative error of at most 0.00096.
Values may be sent and summed in bfloat16 or wider, within the bound.
No kernel may reach another device: no remote copies, remote signals or barrier semaphores. Data moves between devices by JAX's collectives and lax.ppermute only.
A program may use at most 128 MiB of HBM per device.

v0:
```python
import jax
import jax.numpy as jnp
from jax import lax
from jax.sharding import PartitionSpec as P


def with_halo(cells, sides, width):
    for axis, dim in sides:
        count = lax.axis_size(axis)
        ends = count - 1
        head = lax.slice_in_dim(cells, 0, width, axis=dim)
        tail = lax.slice_in_dim(cells, cells.shape[dim] - width, cells.shape[dim], axis=dim)
        cells = jnp.concatenate(
            [
                lax.ppermute(tail, axis, [(i, (i + 1) % count) for i in range(ends)]),
                cells,
                lax.ppermute(head, axis, [((i + 1) % count, i) for i in range(ends)]),
            ],
            axis=dim,
        )
    return cells


def metric_apply(metric, exchanged):
    slab_rows = exchanged[0]
    product = jnp.dot(
        metric, slab_rows.reshape(slab_rows.shape[0], -1), preferred_element_type=jnp.float32
    )
    results = [product.astype(jnp.bfloat16).reshape(slab_rows.shape)]
    return jnp.stack(results)


def add_band(window, gram_block, row_first):
    reach_width = gram_block.shape[0]
    for offset in range(reach_width):
        band_piece = jnp.transpose(gram_block[offset], (1, 0, 2))
        band_piece = jnp.pad(band_piece, ((reach_width - 1 - offset, offset), (0, 0), (0, 0)))
        start_row = row_first + offset
        current = lax.dynamic_slice_in_dim(window, start_row, 1, 0)
        window = lax.dynamic_update_slice_in_dim(window, current + band_piece[None], start_row, 0)
    return window


def body(integrals, orbitals, locality, screen, metric):
    aux_rows, block_count, reach_width, tile_size, _ = integrals.shape
    reach_blocks = reach_width // 2
    orbital_count = orbitals.shape[0]
    per_device = orbital_count // lax.axis_size("aux")
    first_block = lax.axis_index("bas") * block_count
    total_blocks = block_count * lax.axis_size("bas")
    chosen = jnp.take(integrals, locality, axis=1)
    half_rows = lax.dot_general(
        chosen, orbitals, (((4,), (1,)), ((1,), (0,))), preferred_element_type=jnp.float32
    )
    offsets = jnp.arange(reach_width, dtype=jnp.int32)
    row_blocks = first_block + locality[:, None] + offsets[None, :] - reach_blocks
    inside = ((row_blocks >= 0) & (row_blocks < total_blocks)).astype(jnp.float32)
    keep_mask = screen[0].astype(jnp.float32) * inside
    half_rows = (half_rows * keep_mask[:, None, :, None, None]).astype(jnp.bfloat16)
    mixed_rows = metric_apply(
        metric, lax.all_to_all(half_rows, "aux", split_axis=0, concat_axis=1, tiled=True)
    )
    mine = lax.dynamic_slice_in_dim(locality, lax.axis_index("aux") * per_device, per_device, 0)
    window = jnp.zeros(
        (block_count + 2 * reach_blocks, 2 * reach_width - 1, tile_size, tile_size), jnp.float32
    )
    fitted = mixed_rows[0]
    gram_block = lax.dot_general(
        fitted, fitted, (((0, 3), (0, 3)), ((), ())), preferred_element_type=jnp.float32
    )
    window = add_band(window, gram_block, mine[0])
    lower_rim = window[:reach_blocks]
    upper_rim = window[reach_blocks + block_count :]
    own_rows = window[reach_blocks : reach_blocks + block_count]
    both_rims = jnp.concatenate([lower_rim, upper_rim], axis=0)
    extended = with_halo(both_rims.astype(jnp.bfloat16), (("bas", 0),), reach_blocks).astype(
        both_rims.dtype
    )
    from_below = extended[:reach_blocks]
    from_above = extended[3 * reach_blocks :]
    own_rows = own_rows.at[:reach_blocks].add(from_below)
    own_rows = own_rows.at[block_count - reach_blocks :].add(from_above)
    flat_rows = own_rows.reshape(block_count, 2 * reach_width - 1, tile_size * tile_size)
    return lax.psum_scatter(flat_rows, "aux", scatter_dimension=2, tiled=True)


def solution(mesh):
    placed = (
        P("aux", "bas", None, None, None),
        P("bas", None, None),
        P("bas"),
        P("aux", "bas", None),
        P(),
    )
    return jax.shard_map(
        body, mesh=mesh, in_specs=placed, out_specs=P("bas", None, "aux"), check_vma=False
    )
```

profile of v0, /device:TPU:0, one launch (start us, length us, event | category | flops | bytes accessed | tf_op | source)
XLA Modules:
  0.0 197.7 jit_solution(17813742570834771833)
XLA Ops:
  6.5 0.0 copy-start
  6.5 0.8 compare_and_fusion
  7.3 0.7 compare_select_fusion
  8.0 0.7 convert_element_type.33
  8.7 0.1 copy.14
  8.8 0.0 copy-done
  8.8 0.8 gather_fusion
  9.6 2.8 %fusion.8 = bf16[16,1,3,128,128]{4,3,2,1,0:T(8,128)(2,1)} fusion(f32[16,3]{1,0:T(8,128)S(1)} %copy.14, bf16[16,3,128,128]{3,2,1,0:T(8,128)(2,1)S(1)} %gather_fusion, pred[16]{0:T(512)(128)(4,1)S(1)} %compare_and_fusion, bf16[16,128,128]{2,1,0:T(8,128)(2,1)} %param.10), kind=kOutput, calls=%fused_computation.11 | convolution fusion | flops 203685888 | bytes 3670224 | tf_op jit(solution)/shard_map/dot_general | solution.py:52
  12.4 0.0 copy-start.2
  12.4 8.4 %all-to-all-start = ((bf16[16,1,3,128,128]{4,3,2,1,0:T(8,128)(2,1)}), bf16[16,1,3,128,128]{4,3,2,1,0:T(8,128)(2,1)S(1)}, u32[]{:S(2)}, u32[]{:S(2)}) async-start(bf16[16,1,3,128,128]{4,3,2,1,0:T(8,128)(2,1)} %fusion.8), calls=%async_computation | async-start | bytes 3145728 | tf_op jit(solution)/shard_map/all_to_all | solution.py:61
  20.9 0.0 reduce-scatter.2.cloned.1.call-start
  21.0 0.0 copy-done.2
  21.0 0.6 dynamic_slice.9
  26.1 29.0 %all-to-all-done = bf16[16,1,3,128,128]{4,3,2,1,0:T(8,128)(2,1)S(1)} async-done(((bf16[16,1,3,128,128]{4,3,2,1,0:T(8,128)(2,1)}), bf16[16,1,3,128,128]{4,3,2,1,0:T(8,128)(2,1)S(1)}, u32[]{:S(2)}, u32[]{:S(2)}) %all-to-all-start) | async-done | bytes 1572896 | tf_op jit(solution)/shard_map/all_to_all | solution.py:61
  55.1 0.0 copy-done.1
  55.1 1.0 fusion.11
  56.1 0.3 copy.26
  56.4 1.0 fusion.14
  57.4 0.7 broadcast_in_dim.27
  58.2 0.1 fusion.24
  58.3 0.1 fusion.23
  58.3 0.6 convert.6
  59.0 1.3 collective-permute-start
  60.3 1.3 collective-permute-start.1
  61.6 0.6 slice.102
  62.2 0.0 collective-permute-done
  62.3 1.3 collective-permute-done.1
  63.6 0.1 fusion.21
  63.7 2.6 %copy.18 = f32[16,5,128,128]{3,2,0,1:T(8,128)} copy(f32[16,5,128,128]{3,2,1,0:T(8,128)S(1)} %fusion.21) | data formatting | bytes 10485760 | tf_op jit(solution)/shard_map/scatter-add | solution.py:82
  66.3 6.8 %reshape.123 = f32[16,5,16384]{2,0,1:T(8,128)} reshape(f32[16,5,128,128]{3,2,0,1:T(8,128)} %copy.18) | data formatting | bytes 10485760 | tf_op jit(solution)/shard_map/reshape | solution.py:83
  73.1 0.0 reduce-scatter.2.cloned.1.call-update
  73.2 117.7 %reduce-scatter.2.cloned.1.call-done = f32[16,5,1024]{2,0,1:T(8,128)} async-done(((f32[16,5,16384]{2,0,1:T(8,128)}), f32[16,5,1024]{2,0,1:T(8,128)}) %reduce-scatter.2.cloned.1.call-update) | async-done | bytes 327696 | tf_op jit(solution)/shard_map/reduce_scatter | solution.py:84
  (7 shorter events, 0.1 us)
Async XLA Ops:
  6.5 2.2 %copy-start = (bf16[1,16,3,128,128]{4,3,2,1,0:T(8,128)(2,1)S(1)}, bf16[1,16,3,128,128]{4,3,2,1,0:T(8,128)(2,1)}, u32[]{:S(2)}) copy-start(bf16[1,16,3,128,128]{4,3,2,1,0:T(8,128)(2,1)} %param.9) | copy-start | bytes 4718596
  12.4 8.5 %copy-start.2 = (s32[16]{0:T(128)S(1)}, s32[16]{0:T(128)}, u32[]{:S(2)}) copy-start(s32[16]{0:T(128)} %param.11) | copy-start | bytes 196
  12.4 42.6 %copy-start.1 = (bf16[16,16]{1,0:T(8,128)(2,1)S(1)}, bf16[16,16]{1,0:T(8,128)(2,1)}, u32[]{:S(2)}) copy-start(bf16[16,16]{1,0:T(8,128)(2,1)} %param.13) | copy-start | bytes 1540
  12.4 42.6 %all-to-all-start = ((bf16[16,1,3,128,128]{4,3,2,1,0:T(8,128)(2,1)}), bf16[16,1,3,128,128]{4,3,2,1,0:T(8,128)(2,1)S(1)}, u32[]{:S(2)}, u32[]{:S(2)}) async-start(bf16[16,1,3,128,128]{4,3,2,1,0:T(8,128)(2,1)} %fusion.8), calls=%async_computation | async-start | bytes 3145728 | tf_op jit(solution)/shard_map/all_to_all | solution.py:61
  20.9 169.9 %reduce-scatter.2.cloned.1.call-start = ((), (), s32[]{:S(2)}) async-start(), calls=%async_computation.2 | async-start | bytes 5570560 | tf_op jit(solution)/shard_map/reduce_scatter | solution.py:84
  59.0 3.3 %collective-permute-start = (bf16[1,5,128,128]{3,2,1,0:T(8,128)(2,1)S(1)}, bf16[1,5,128,128]{3,2,1,0:T(8,128)(2,1)S(1)}, u32[]{:S(2)}, u32[]{:S(2)}) collective-permute-start(bf16[1,5,128,128]{3,2,1,0:T(8,128)(2,1)S(1)} %get-tuple-element.29), channel_id=1, source_target_pairs={{0,1},{2,3},{4,5},{6,7},{8,9},{10,11},{12,13},{14,15},{16,17},{18,... | collective-permute-start | bytes 491528 | tf_op jit(solution)/shard_map/ppermute | solution.py:15
  60.3 3.3 %collective-permute-start.1 = (bf16[1,5,128,128]{3,2,1,0:T(8,128)(2,1)S(1)}, bf16[1,5,128,128]{3,2,1,0:T(8,128)(2,1)S(1)}, u32[]{:S(2)}, u32[]{:S(2)}) collective-permute-start(bf16[1,5,128,128]{3,2,1,0:T(8,128)(2,1)S(1)} %get-tuple-element.30), channel_id=1, source_target_pairs={{1,0},{3,2},{5,4},{7,6},{9,8},{11,10},{13,12},{15,14},{17,16},{19,... | collective-permute-start | bytes 491528 | tf_op jit(solution)/shard_map/ppermute | solution.py:17
Sparse Core Ops, SparseCore 0:
  73.3 117.4 reduce-scatter.1
where the time goes:
time: 198 us
  waiting for transfers between devices  148 us (75%)
  between operations  18.1 us (9%)
  local copies, waits for them, and re-layouts  12.7 us (6%)
  starting transfers between devices  11.1 us (6%)
  matrix products  4.83 us (2%)
  other arithmetic  2.97 us (2%)
    reduce_scatter x1, waiting for transfers between devices, body(): return lax.psum_scatter(flat_rows, 'aux', scatter_dimension=2, tiled=True)  118 us
    all_to_all x1, waiting for transfers between devices, body(): lax.all_to_all(half_rows, 'aux', split_axis=0, concat_axis=1, tiled=True)  29 us
    all_to_all x1, starting transfers between devices, body(): lax.all_to_all(half_rows, 'aux', split_axis=0, concat_axis=1, tiled=True)  8.44 us
    reshape x1, local copies, waits for them, and re-layouts, body(): own_rows.reshape(block_count, 2 * reach_width - 1, tile_size * tile_size)  6.79 us
  transfers between devices with their start and end apart: 4, of which 3 were waited for; matrix products, arithmetic and copies ran while one was open for 1% of the time, Pallas kernels for 0%

commit v1 on v0

v1 whole, which is shorter than its diff:
```python
import functools

import jax
import jax.numpy as jnp
from jax import lax
from jax.experimental import pallas as pl
from jax.experimental.pallas import tpu as pltpu
from jax.sharding import PartitionSpec as P

ROWS = 8
LEVELS = 32000.0
STEPS = 128.0
FAST = pltpu.CompilerParams(vmem_limit_bytes=48 * 1024 * 1024)


def half_kernel(locality, screen, integrals, orbitals, half, taken, given, in_sem, out_sem):
    tiles, reach, tile, _ = taken.shape
    total = tiles * lax.axis_size("bas")
    first = lax.axis_index("bas") * tiles

    def fetch(j):
        return pltpu.make_async_copy(integrals.at[0, locality[j]], taken.at[j], in_sem.at[j])

    def give(j):
        return pltpu.make_async_copy(given.at[j], half.at[locality[j]], out_sem.at[j])

    for j in range(tiles):
        fetch(j).start()
    for j in range(tiles):
        fetch(j).wait()
        product = jnp.dot(
            taken[j].reshape(reach * tile, tile), orbitals[j], preferred_element_type=jnp.float32
        )
        for d in range(reach):
            block = first + locality[j] + d - reach // 2
            inside = (block >= 0) & (block < total)
            keep = jnp.where(inside, screen[0, j, d], 0).astype(jnp.float32)
            given[j, d] = (product[d * tile : (d + 1) * tile] * keep).astype(jnp.bfloat16)
        give(j).start()
    for j in range(tiles):
        give(j).wait()


def gram_kernel(metric, rows, coded, taken, fitted, in_sem):
    aux, reach, tile, _ = taken.shape
    group = 16

    def fetch(d):
        return pltpu.make_async_copy(rows.at[:, d], taken.at[:, d], in_sem.at[d])

    for d in range(reach):
        fetch(d).start()
    wide = aux * group
    spread = (
        lax.broadcasted_iota(jnp.int32, (wide, aux), 0) // group
        == lax.broadcasted_iota(jnp.int32, (wide, aux), 1)
    ).astype(jnp.bfloat16)
    picked = jnp.dot(spread, metric[...], preferred_element_type=jnp.float32).astype(jnp.bfloat16)
    mixer = lax.dot_general(
        picked, spread, (((1,), (1,)), ((), ())), preferred_element_type=jnp.float32
    )
    same_row = (
        lax.broadcasted_iota(jnp.int32, (wide, wide), 0) % group
        == lax.broadcasted_iota(jnp.int32, (wide, wide), 1) % group
    )
    mixer = jnp.where(same_row, mixer, 0.0).astype(jnp.bfloat16)
    for d in range(reach):
        fetch(d).wait()
        for g in range(0, tile, 2 * group):
            pair = [
                taken[:, d, g + s * group : g + (s + 1) * group, :].reshape(wide, tile)
                for s in range(2)
            ]
            mixed = jnp.dot(
                mixer, jnp.concatenate(pair, axis=1), preferred_element_type=jnp.float32
            ).astype(jnp.bfloat16)
            for s in range(2):
                start = d * tile + g + s * group
                for q in range(aux):
                    fitted[start : start + group, q * tile : (q + 1) * tile] = mixed[
                        q * group : (q + 1) * group, s * tile : (s + 1) * tile
                    ]
    gram = lax.dot_general(
        fitted[...], fitted[...], (((1,), (1,)), ((), ())), preferred_element_type=jnp.float32
    )
    lane = lax.broadcasted_iota(jnp.int32, (ROWS, tile), 1)
    owners = coded.shape[0]
    per = tile // owners
    for a in range(owners):
        codes, scales = [], jnp.zeros((ROWS, tile), jnp.float32)
        for d in range(reach):
            for d2 in range(reach):
                block = gram[
                    d * tile + a * per : d * tile + (a + 1) * per, d2 * tile : (d2 + 1) * tile
                ]
                if per < ROWS:
                    block = jnp.concatenate(
                        [block, jnp.zeros((ROWS - per, tile), jnp.float32)], axis=0
                    )
                code, scale = encode(block)
                codes.append(code)
                scales = jnp.where(lane == d * reach + d2, scale, scales)
        sent = jnp.concatenate(codes + [scales], axis=0)
        coded[a] = sent.astype(jnp.int32).astype(jnp.int16)


def encode(block):
    peak = jnp.max(jnp.abs(block), axis=1, keepdims=True)
    scale = jnp.ceil(jnp.log2(jnp.maximum(peak, 1e-37)) * STEPS)
    return jnp.round(block * (jnp.exp2(scale * (-1.0 / STEPS)) * LEVELS)), scale


def decode(codes, scales, which):
    factor = jnp.exp2(scales[:, which : which + 1] * (1.0 / STEPS)) * (1.0 / LEVELS)
    return codes[which * ROWS : (which + 1) * ROWS] * factor


def band_kernel(reach, received, rim, band):
    centres, height, tile = received.shape
    per = band.shape[2] // tile
    offsets = 2 * reach - 1
    middle = reach // 2
    on_first = lax.axis_index("bas") == 0
    sums = {}

    def add(m, e, piece):
        sums[m, e] = sums[m, e] + piece if (m, e) in sums else piece

    def finish(m):
        for e in range(offsets):
            total = sums.pop((m, e), jnp.zeros((ROWS, tile), jnp.float32))
            for r in range(per):
                band[m, e : e + 1, r * tile : (r + 1) * tile] = total[r : r + 1]

    beside = rim[0].astype(jnp.int32).astype(jnp.float32)
    beside_scales = beside[reach * reach * ROWS :]
    for d2 in range(reach):
        low = decode(beside, beside_scales, (reach - 1) * reach + d2)
        add(0, d2, jnp.where(on_first, 0.0, low))
        high = decode(beside, beside_scales, d2)
        add(centres - 1, d2 + reach - 1, jnp.where(on_first, high, 0.0))
    for c in range(centres):
        tile_codes = received[c].astype(jnp.int32).astype(jnp.float32)
        scales = tile_codes[reach * reach * ROWS :]
        for d in range(reach):
            m = c + d - middle
            if 0 <= m < centres:
                for d2 in range(reach):
                    add(m, d2 - d + reach - 1, decode(tile_codes, scales, d * reach + d2))
        if c >= middle:
            finish(c - middle)
    for m in range(centres - middle, centres):
        finish(m)


def body(integrals, orbitals, locality, screen, metric):
    _, tiles, reach, tile, _ = integrals.shape
    aux = lax.axis_size("aux")
    if lax.axis_size("bas") != 2 or tiles != aux or reach != 3:
        raise ValueError("unsupported sizes")
    any_space = pl.BlockSpec(memory_space=pl.ANY)
    scalars = pl.BlockSpec(memory_space=pltpu.SMEM)
    vectors = pl.BlockSpec(memory_space=pltpu.VMEM)
    half = pl.pallas_call(
        half_kernel,
        out_shape=jax.ShapeDtypeStruct((tiles, reach, tile, tile), jnp.bfloat16),
        in_specs=[scalars, scalars, any_space, vectors],
        out_specs=any_space,
        scratch_shapes=[
            pltpu.VMEM((tiles, reach, tile, tile), jnp.bfloat16),
            pltpu.VMEM((tiles, reach, tile, tile), jnp.bfloat16),
            pltpu.SemaphoreType.DMA((tiles,)),
            pltpu.SemaphoreType.DMA((tiles,)),
        ],
        compiler_params=FAST,
        name="half_transform",
    )(locality, screen, integrals, orbitals)
    rows = lax.all_to_all(half, "aux", split_axis=0, concat_axis=0, tiled=True)
    coded = pl.pallas_call(
        gram_kernel,
        out_shape=jax.ShapeDtypeStruct((aux, (reach * reach + 1) * ROWS, tile), jnp.int16),
        in_specs=[vectors, any_space],
        out_specs=vectors,
        scratch_shapes=[
            pltpu.VMEM((aux, reach, tile, tile), jnp.bfloat16),
            pltpu.VMEM((reach * tile, aux * tile), jnp.bfloat16),
            pltpu.SemaphoreType.DMA((reach,)),
        ],
        compiler_params=FAST,
        name="fit_and_gram",
    )(metric, rows)
    received = lax.all_to_all(coded, "aux", split_axis=0, concat_axis=0, tiled=True)
    edge = jnp.where(lax.axis_index("bas") == 0, tiles - 1, 0)
    edge_tile = lax.dynamic_slice_in_dim(received, edge, 1, 0)
    rim = lax.ppermute(edge_tile, "bas", [(0, 1), (1, 0)])
    return pl.pallas_call(
        functools.partial(band_kernel, reach),
        out_shape=jax.ShapeDtypeStruct(
            (tiles, 2 * reach - 1, tile * tile // aux), jnp.float32
        ),
        in_specs=[vectors, vectors],
        out_specs=vectors,
        compiler_params=FAST,
        name="band_sum",
    )(received, rim)


def solution(mesh):
    placed = (
        P("aux", "bas", None, None, None),
        P("bas", None, None),
        P("bas"),
        P("aux", "bas", None),
        P(),
    )
    return jax.shard_map(
        body, mesh=mesh, in_specs=placed, out_specs=P("bas", None, "aux"), check_vma=False
    )
```

time: 198 us -> 78 us (0.39)
  waiting for transfers between devices: 148 us -> 11.7 us
  blocking collectives: 0 us -> 45.7 us
  between operations: 18.1 us -> 0.05 us
  Pallas kernels: 0 us -> 11.4 us
  local copies, waits for them, and re-layouts: 12.7 us -> 4.79 us
  starting transfers between devices: 11.1 us -> 3.91 us
  matrix products: 4.83 us -> 0 us
  other arithmetic: 2.97 us -> 0 us
    reduce_scatter x1 -> x0, waiting for transfers between devices: 118 us -> none  [body(): return lax.psum_scatter(flat_rows, 'aux', scatter_dimension=2, tiled=True)]
    all_to_all x0 -> x1, blocking collectives: none -> 45.7 us  [body(): rows = lax.all_to_all(half, 'aux', split_axis=0, concat_axis=0, tiled=True)]
    all_to_all x1, waiting for transfers between devices: 29 us -> 10.5 us  [body(): lax.all_to_all(coded, 'aux', split_axis=0, concat_axis=0, tiled=True)]
    pallas_call x0 -> x3, Pallas kernels: none -> 11.4 us  [the longest x1 7.99 us: body(): pl.pallas_call(half_kernel, out_shape=jax.ShapeDtypeStruct((tiles, reach,...]
    reshape x1 -> x0, local copies, waits for them, and re-layouts: 6.79 us -> none  [body(): own_rows.reshape(block_count, 2 * reach_width - 1, tile_size * tile_size)]
    dot_general x3 -> x0, matrix products: 4.83 us -> none  [the longest x1 2.83 us: body(): lax.dot_general(chosen, orbitals, (((4,), (1,)), ((1,), (0,))), preferred...]
    all_to_all x1, starting transfers between devices: 8.44 us -> 3.9 us  [body(): lax.all_to_all(coded, 'aux', split_axis=0, concat_axis=0, tiled=True)]
    unnamed x7 -> x9, local copies, waits for them, and re-layouts: 0.3 us -> 3.87 us
  transfers between devices with their start and end apart: 4 -> 2, of which waited for: 3 -> 2; matrix products, arithmetic and copies ran while one was open for 1% -> 0% of each run, Pallas kernels for 0% -> 0%
where the time goes in v1:
time: 78 us; the launch traced here: 77.6 us
  blocking collectives  45.7 us (59%)
  waiting for transfers between devices  11.7 us (15%)
  Pallas kernels  11.4 us (15%)
  local copies, waits for them, and re-layouts  4.79 us (6%)
  starting transfers between devices  3.91 us (5%)
    all_to_all x1, blocking collectives, body(): rows = lax.all_to_all(half, 'aux', split_axis=0, concat_axis=0, tiled=True)  45.7 us
    all_to_all x1, waiting for transfers between devices, body(): lax.all_to_all(coded, 'aux', split_axis=0, concat_axis=0, tiled=True)  10.5 us
    pallas_call x1, Pallas kernels, body(): pl.pallas_call(half_kernel, out_shape=jax.ShapeDtypeStruct((tiles, reach,...  7.99 us
    all_to_all x1, starting transfers between devices, body(): lax.all_to_all(coded, 'aux', split_axis=0, concat_axis=0, tiled=True)  3.9 us
    unnamed x9, local copies, waits for them, and re-layouts  3.87 us
    pallas_call x1, Pallas kernels, body(): pl.pallas_call(gram_kernel, out_shape=jax.ShapeDtypeStruct((aux, (reach *...  3.11 us
  transfers between devices with their start and end apart: 2, of which 2 were waited for; matrix products, arithmetic and copies ran while one was open for 0% of the time, Pallas kernels for 0%

profile of v1, /device:TPU:0, one launch (start us, length us, event | category | flops | bytes accessed | tf_op | source)
XLA Modules:
  0.0 77.6 jit_solution(12183342970440215912)
XLA Ops:
  0.0 0.8 copy.6.screen
  0.8 0.0 copy-start
  0.8 1.4 %copy-done = bf16[1,16,3,128,128]{4,3,2,1,0:T(8,128)(2,1)S(1)} copy-done((bf16[1,16,3,128,128]{4,3,2,1,0:T(8,128)(2,1)S(1)}, bf16[1,16,3,128,128]{4,3,2,1,0:T(8,128)(2,1)}, u32[]{:S(2)}) %copy-start) | copy-done | bytes 1572888
  2.2 0.0 copy-start.1
  2.2 1.0 %copy-done.1 = bf16[16,128,128]{2,1,0:T(8,128)(2,1)S(1)} copy-done((bf16[16,128,128]{2,1,0:T(8,128)(2,1)S(1)}, bf16[16,128,128]{2,1,0:T(8,128)(2,1)}, u32[]{:S(2)}) %copy-start.1) | copy-done | bytes 524312
  3.2 0.0 copy-start.3
  3.2 0.7 copy-done.3
  3.9 8.0 %half_transform.1 = bf16[16,3,128,128]{3,2,1,0:T(8,128)(2,1)S(1)} custom-call(s32[16]{0:T(128)S(1)} %copy-done.3, s32[1,16,3]{2,1,0:T(8,128)S(1)} %copy.6.screen, bf16[1,16,3,128,128]{4,3,2,1,0:T(8,128)(2,1)S(1)} %copy-done, bf16[16,128,128]{2,1,0:T(8,128)(2,1)S(1)} %copy-done.1), custom_call_target="tpu_custom_call" | custom-call | tf_op jit(solution)/shard_map/half_transform/pallas_call | solution.py:164
  11.9 0.0 copy-start.2
  11.9 45.7 %all_to_all.10.rows = bf16[16,3,128,128]{3,2,1,0:T(8,128)(2,1)S(1)} all-to-all(bf16[16,3,128,128]{3,2,1,0:T(8,128)(2,1)S(1)} %half_transform.1), channel_id=1, replica_groups=mesh['aux'=16,'bas'=2] {'aux'}, dimensions={0} | all-to-all | bytes 3145728 | tf_op jit(solution)/shard_map/all_to_all | solution.py:178
  57.6 0.0 copy-done.2
  57.6 3.1 %fit_and_gram.1 = s16[16,80,128]{2,1,0:T(8,128)(2,1)} custom-call(bf16[16,16]{1,0:T(8,128)(2,1)S(1)} %copy-done.2, bf16[16,3,128,128]{3,2,1,0:T(8,128)(2,1)S(1)} %all_to_all.10.rows), custom_call_target="tpu_custom_call" | custom-call | tf_op jit(solution)/shard_map/fit_and_gram/pallas_call | solution.py:179
  60.7 3.9 %all-to-all-start.1 = ((s16[16,80,128]{2,1,0:T(8,128)(2,1)}), s16[16,80,128]{2,1,0:T(8,128)(2,1)S(1)}, u32[]{:S(2)}, u32[]{:S(2)}) async-start(s16[16,80,128]{2,1,0:T(8,128)(2,1)} %fit_and_gram.1), calls=%async_computation.1 | async-start | bytes 655360 | tf_op jit(solution)/shard_map/all_to_all | solution.py:192
  64.6 10.5 %all-to-all-done.1.received = s16[16,80,128]{2,1,0:T(8,128)(2,1)S(1)} async-done(((s16[16,80,128]{2,1,0:T(8,128)(2,1)}), s16[16,80,128]{2,1,0:T(8,128)(2,1)S(1)}, u32[]{:S(2)}, u32[]{:S(2)}) %all-to-all-start.1) | async-done | bytes 327712 | tf_op jit(solution)/shard_map/all_to_all | solution.py:192
  75.2 0.0 collective-permute-start
  75.2 1.2 %collective-permute-done.rim = s16[1,80,128]{2,1,0:T(8,128)(2,1)S(1)} collective-permute-done((s16[1,80,128]{2,1,0:T(8,128)(2,1)S(1)}, s16[1,80,128]{2,1,0:T(8,128)(2,1)S(1)}, u32[]{:S(2)}, u32[]{:S(2)}) %collective-permute-start) | collective-permute-done | bytes 20512 | tf_op jit(solution)/shard_map/ppermute | solution.py:195
  76.4 0.3 band_sum.1
  76.7 0.9 %copy.7 = f32[16,5,1024]{2,0,1:T(8,128)} copy(f32[16,5,1024]{2,1,0:T(8,128)S(1)} %band_sum.1) | data formatting | bytes 655360 | tf_op jit(solution)/shard_map/band_sum/pallas_call | solution.py:196
  (1 shorter events, 0.0 us)
Async XLA Ops:
  0.8 1.4 %copy-start = (bf16[1,16,3,128,128]{4,3,2,1,0:T(8,128)(2,1)S(1)}, bf16[1,16,3,128,128]{4,3,2,1,0:T(8,128)(2,1)}, u32[]{:S(2)}) copy-start(bf16[1,16,3,128,128]{4,3,2,1,0:T(8,128)(2,1)} %integrals.1) | copy-start | bytes 4718596
  2.2 1.0 %copy-start.1 = (bf16[16,128,128]{2,1,0:T(8,128)(2,1)S(1)}, bf16[16,128,128]{2,1,0:T(8,128)(2,1)}, u32[]{:S(2)}) copy-start(bf16[16,128,128]{2,1,0:T(8,128)(2,1)} %orbitals.1) | copy-start | bytes 1572868
  3.2 0.7 copy-start.3
  11.9 45.7 %copy-start.2 = (bf16[16,16]{1,0:T(8,128)(2,1)S(1)}, bf16[16,16]{1,0:T(8,128)(2,1)}, u32[]{:S(2)}) copy-start(bf16[16,16]{1,0:T(8,128)(2,1)} %metric.1) | copy-start | bytes 1540
  60.7 14.5 %all-to-all-start.1 = ((s16[16,80,128]{2,1,0:T(8,128)(2,1)}), s16[16,80,128]{2,1,0:T(8,128)(2,1)S(1)}, u32[]{:S(2)}, u32[]{:S(2)}) async-start(s16[16,80,128]{2,1,0:T(8,128)(2,1)} %fit_and_gram.1), calls=%async_computation.1 | async-start | bytes 655360 | tf_op jit(solution)/shard_map/all_to_all | solution.py:192
  75.2 1.2 %collective-permute-start = (s16[1,80,128]{2,1,0:T(8,128)(2,1)S(1)}, s16[1,80,128]{2,1,0:T(8,128)(2,1)S(1)}, u32[]{:S(2)}, u32[]{:S(2)}) collective-permute-start(s16[1,80,128]{2,1,0:T(8,128)(2,1)S(1)} %constant_dynamic-slice_fusion), channel_id=1, source_target_pairs={{0,1},{1,0},{2,3},{3,2},{4,5},{5,4},{6,7},{7,6},{8,9},{9,8},{10,11... | collective-permute-start | bytes 61448 | tf_op jit(solution)/shard_map/ppermute | solution.py:195

commit v2 on v1

--- a/solution.py
+++ b/solution.py
@@ -9,47 +9,55 @@
 
 ROWS = 8
 LEVELS = 32000.0
+PARTS = 4
 STEPS = 128.0
 FAST = pltpu.CompilerParams(vmem_limit_bytes=48 * 1024 * 1024)
 
 
-def half_kernel(locality, screen, integrals, orbitals, half, taken, given, in_sem, out_sem):
+def half_kernel(
+    locality, screen, integrals, orbitals, half, taken, factors, places, flags, owner, sems
+):
     tiles, reach, tile, _ = taken.shape
     total = tiles * lax.axis_size("bas")
     first = lax.axis_index("bas") * tiles
-
-    def fetch(j):
-        return pltpu.make_async_copy(integrals.at[0, locality[j]], taken.at[j], in_sem.at[j])
-
-    def give(j):
-        return pltpu.make_async_copy(given.at[j], half.at[locality[j]], out_sem.at[j])
-
+    part = max(tiles // PARTS, 1)
+    small = [
+        pltpu.make_async_copy(locality, places, sems.at[0]),
+        pltpu.make_async_copy(screen, flags, sems.at[1]),
+        pltpu.make_async_copy(orbitals, factors, sems.at[2]),
+    ]
+    blocks = [
+        pltpu.make_async_copy(
+            integrals.at[0, pl.ds(start, part)], taken.at[pl.ds(start, part)], sems.at[3 + k]
+        )
+        for k, start in enumerate(range(0, tiles, part))
+    ]
+    for copy in small + blocks:
+        copy.start()
+    small[0].wait()
     for j in range(tiles):
-        fetch(j).start()
-    for j in range(tiles):
-        fetch(j).wait()
-        product = jnp.dot(
-            taken[j].reshape(reach * tile, tile), orbitals[j], preferred_element_type=jnp.float32
-        )
-        for d in range(reach):
-            block = first + locality[j] + d - reach // 2
-            inside = (block >= 0) & (block < total)
-            keep = jnp.where(inside, screen[0, j, d], 0).astype(jnp.float32)
-            given[j, d] = (product[d * tile : (d + 1) * tile] * keep).astype(jnp.bfloat16)
-        give(j).start()
-    for j in range(tiles):
-        give(j).wait()
-
-
-def gram_kernel(metric, rows, coded, taken, fitted, in_sem):
-    aux, reach, tile, _ = taken.shape
+        owner[places[j]] = j
+    small[1].wait()
+    small[2].wait()
+    for k, copy in enumerate(blocks):
+        copy.wait()
+        for c in range(k * part, (k + 1) * part):
+            j = owner[c]
+            product = jnp.dot(
+                taken[c].reshape(reach * tile, tile),
+                factors[j],
+                preferred_element_type=jnp.float32,
+            )
+            for d in range(reach):
+                block = first + c + d - reach // 2
+                inside = (block >= 0) & (block < total)
+                keep = jnp.where(inside, flags[d, 0, j], 0).astype(jnp.float32)
+                half[c, d] = (product[d * tile : (d + 1) * tile] * keep).astype(jnp.bfloat16)
+
+
+def gram_kernel(metric, rows, coded, fitted):
+    aux, reach, tile, _ = rows.shape
     group = 16
-
-    def fetch(d):
-        return pltpu.make_async_copy(rows.at[:, d], taken.at[:, d], in_sem.at[d])
-
-    for d in range(reach):
-        fetch(d).start()
     wide = aux * group
     spread = (
         lax.broadcasted_iota(jnp.int32, (wide, aux), 0) // group
@@ -65,10 +73,9 @@
     )
     mixer = jnp.where(same_row, mixer, 0.0).astype(jnp.bfloat16)
     for d in range(reach):
-        fetch(d).wait()
         for g in range(0, tile, 2 * group):
             pair = [
-                taken[:, d, g + s * group : g + (s + 1) * group, :].reshape(wide, tile)
+                rows[:, d, g + s * group : g + (s + 1) * group, :].reshape(wide, tile)
                 for s in range(2)
             ]
             mixed = jnp.dot(
@@ -116,7 +123,7 @@
 
 
 def band_kernel(reach, received, rim, band):
-    centres, height, tile = received.shape
+    centres, _, tile = received.shape
     per = band.shape[2] // tile
     offsets = 2 * reach - 1
     middle = reach // 2
@@ -130,7 +137,7 @@
         for e in range(offsets):
             total = sums.pop((m, e), jnp.zeros((ROWS, tile), jnp.float32))
             for r in range(per):
-                band[m, e : e + 1, r * tile : (r + 1) * tile] = total[r : r + 1]
+                band[e, m : m + 1, r * tile : (r + 1) * tile] = total[r : r + 1]
 
     beside = rim[0].astype(jnp.int32).astype(jnp.float32)
     beside_scales = beside[reach * reach * ROWS :]
@@ -158,33 +165,35 @@
     aux = lax.axis_size("aux")
     if lax.axis_size("bas") != 2 or tiles != aux or reach != 3:
         raise ValueError("unsupported sizes")
-    any_space = pl.BlockSpec(memory_space=pl.ANY)
-    scalars = pl.BlockSpec(memory_space=pltpu.SMEM)
+    main_memory = pl.BlockSpec(memory_space=pltpu.HBM)
     vectors = pl.BlockSpec(memory_space=pltpu.VMEM)
     half = pl.pallas_call(
         half_kernel,
         out_shape=jax.ShapeDtypeStruct((tiles, reach, tile, tile), jnp.bfloat16),
-        in_specs=[scalars, scalars, any_space, vectors],
-        out_specs=any_space,
+        in_specs=[main_memory] * 4,
+        out_specs=vectors,
         scratch_shapes=[
             pltpu.VMEM((tiles, reach, tile, tile), jnp.bfloat16),
-            pltpu.VMEM((tiles, reach, tile, tile), jnp.bfloat16),
-            pltpu.SemaphoreType.DMA((tiles,)),
-            pltpu.SemaphoreType.DMA((tiles,)),
+            pltpu.VMEM((tiles, tile, tile), jnp.bfloat16),
+            pltpu.SMEM((tiles,), jnp.int32),
+            pltpu.SMEM((reach, 1, tiles), jnp.int32),
+            pltpu.SMEM((tiles,), jnp.int32),
+            pltpu.SemaphoreType.DMA((3 + PARTS,)),
         ],
         compiler_params=FAST,
         name="half_transform",
-    )(locality, screen, integrals, orbitals)
+    )(*(
+        pltpu.with_memory_space_constraint(array, pltpu.HBM)
+        for array in (locality, jnp.transpose(screen, (2, 0, 1)), integrals, orbitals)
+    ))
     rows = lax.all_to_all(half, "aux", split_axis=0, concat_axis=0, tiled=True)
     coded = pl.pallas_call(
         gram_kernel,
         out_shape=jax.ShapeDtypeStruct((aux, (reach * reach + 1) * ROWS, tile), jnp.int16),
-        in_specs=[vectors, any_space],
+        in_specs=[vectors, vectors],
         out_specs=vectors,
         scratch_shapes=[
-            pltpu.VMEM((aux, reach, tile, tile), jnp.bfloat16),
             pltpu.VMEM((reach * tile, aux * tile), jnp.bfloat16),
-            pltpu.SemaphoreType.DMA((reach,)),
         ],
         compiler_params=FAST,
         name="fit_and_gram",
@@ -193,16 +202,17 @@
     edge = jnp.where(lax.axis_index("bas") == 0, tiles - 1, 0)
     edge_tile = lax.dynamic_slice_in_dim(received, edge, 1, 0)
     rim = lax.ppermute(edge_tile, "bas", [(0, 1), (1, 0)])
-    return pl.pallas_call(
+    band = pl.pallas_call(
         functools.partial(band_kernel, reach),
         out_shape=jax.ShapeDtypeStruct(
-            (tiles, 2 * reach - 1, tile * tile // aux), jnp.float32
+            (2 * reach - 1, tiles, tile * tile // aux), jnp.float32
         ),
         in_specs=[vectors, vectors],
         out_specs=vectors,
         compiler_params=FAST,
         name="band_sum",
     )(received, rim)
+    return jnp.transpose(band, (1, 0, 2))
 
 
 def solution(mesh):

time: 78 us -> 67.5 us (0.87)
  Pallas kernels: 11.4 us -> 5.86 us
  local copies, waits for them, and re-layouts: 4.79 us -> 0.01 us
    pallas_call x1, Pallas kernels: 7.99 us -> 2.24 us  [body(): pl.pallas_call(half_kernel, out_shape=jax.ShapeDtypeStruct((tiles, reach,...]
    unnamed x9 -> x2, local copies, waits for them, and re-layouts: 3.87 us -> 0.01 us
    pallas_call x1 -> x0, local copies, waits for them, and re-layouts: 0.92 us -> none  [body(): pl.pallas_call(functools.partial(band_kernel, reach), out_shape=jax.Shape...]
where the time goes in v2:
time: 67.5 us; the launch traced here: 67.3 us
  blocking collectives  45.7 us (68%)
  waiting for transfers between devices  11.7 us (17%)
  Pallas kernels  5.86 us (9%)
  starting transfers between devices  3.89 us (6%)
    all_to_all x1, blocking collectives, body(): rows = lax.all_to_all(half, 'aux', split_axis=0, concat_axis=0, tiled=True)  45.7 us
    all_to_all x1, waiting for transfers between devices, body(): lax.all_to_all(coded, 'aux', split_axis=0, concat_axis=0, tiled=True)  10.5 us
    all_to_all x1, starting transfers between devices, body(): lax.all_to_all(coded, 'aux', split_axis=0, concat_axis=0, tiled=True)  3.89 us
    pallas_call x1, Pallas kernels, body(): pl.pallas_call(gram_kernel, out_shape=jax.ShapeDtypeStruct((aux, (reach *...  2.55 us
    pallas_call x1, Pallas kernels, body(): pl.pallas_call(half_kernel, out_shape=jax.ShapeDtypeStruct((tiles, reach,...  2.24 us
  transfers between devices with their start and end apart: 2, of which 2 were waited for; matrix products, arithmetic and copies ran while one was open for 0% of the time, Pallas kernels for 0%

profile of v2, /device:TPU:0, one launch (start us, length us, event | category | flops | bytes accessed | tf_op | source)
XLA Modules:
  0.0 67.3 jit_solution(14149427472627436063)
XLA Ops:
  0.0 2.2 %half_transform.1 = bf16[16,3,128,128]{3,2,1,0:T(8,128)(2,1)S(1)} custom-call(s32[16]{0:T(128)} %locality.1, s32[3,1,16]{2,1,0:T(1,128)} %bitcast.2, bf16[1,16,3,128,128]{4,3,2,1,0:T(8,128)(2,1)} %integrals.1, bf16[16,128,128]{2,1,0:T(8,128)(2,1)} %orbitals.1), custom_call_target="tpu_custom_call" | custom-call | tf_op jit(solution)/shard_map/half_transform/pallas_call | solution.py:170
  2.2 0.0 copy-start
  2.3 45.7 %all_to_all.10.rows = bf16[16,3,128,128]{3,2,1,0:T(8,128)(2,1)S(1)} all-to-all(bf16[16,3,128,128]{3,2,1,0:T(8,128)(2,1)S(1)} %half_transform.1), channel_id=1, replica_groups=mesh['aux'=16,'bas'=2] {'aux'}, dimensions={0} | all-to-all | bytes 3145728 | tf_op jit(solution)/shard_map/all_to_all | solution.py:189
  48.0 0.0 copy-done
  48.0 2.6 %fit_and_gram.1 = s16[16,80,128]{2,1,0:T(8,128)(2,1)} custom-call(bf16[16,16]{1,0:T(8,128)(2,1)S(1)} %copy-done, bf16[16,3,128,128]{3,2,1,0:T(8,128)(2,1)S(1)} %all_to_all.10.rows), custom_call_target="tpu_custom_call" | custom-call | tf_op jit(solution)/shard_map/fit_and_gram/pallas_call | solution.py:190
  50.5 3.9 %all-to-all-start.1 = ((s16[16,80,128]{2,1,0:T(8,128)(2,1)}), s16[16,80,128]{2,1,0:T(8,128)(2,1)S(1)}, u32[]{:S(2)}, u32[]{:S(2)}) async-start(s16[16,80,128]{2,1,0:T(8,128)(2,1)} %fit_and_gram.1), calls=%async_computation.1 | async-start | bytes 655360 | tf_op jit(solution)/shard_map/all_to_all | solution.py:201
  54.4 10.5 %all-to-all-done.1.received = s16[16,80,128]{2,1,0:T(8,128)(2,1)S(1)} async-done(((s16[16,80,128]{2,1,0:T(8,128)(2,1)}), s16[16,80,128]{2,1,0:T(8,128)(2,1)S(1)}, u32[]{:S(2)}, u32[]{:S(2)}) %all-to-all-start.1) | async-done | bytes 327712 | tf_op jit(solution)/shard_map/all_to_all | solution.py:201
  65.0 0.0 collective-permute-start
  65.0 1.2 %collective-permute-done.rim = s16[1,80,128]{2,1,0:T(8,128)(2,1)S(1)} collective-permute-done((s16[1,80,128]{2,1,0:T(8,128)(2,1)S(1)}, s16[1,80,128]{2,1,0:T(8,128)(2,1)S(1)}, u32[]{:S(2)}, u32[]{:S(2)}) %collective-permute-start) | collective-permute-done | bytes 20512 | tf_op jit(solution)/shard_map/ppermute | solution.py:204
  66.2 1.1 %band_sum.1 = f32[5,16,1024]{2,1,0:T(8,128)} custom-call(s16[16,80,128]{2,1,0:T(8,128)(2,1)S(1)} %all-to-all-done.1.received, s16[1,80,128]{2,1,0:T(8,128)(2,1)S(1)} %collective-permute-done.rim), custom_call_target="tpu_custom_call" | custom-call | tf_op jit(solution)/shard_map/band_sum/pallas_call | solution.py:205
  (1 shorter events, 0.0 us)
Async XLA Ops:
  2.2 45.7 %copy-start = (bf16[16,16]{1,0:T(8,128)(2,1)S(1)}, bf16[16,16]{1,0:T(8,128)(2,1)}, u32[]{:S(2)}) copy-start(bf16[16,16]{1,0:T(8,128)(2,1)} %metric.1) | copy-start | bytes 1540
  50.5 14.5 %all-to-all-start.1 = ((s16[16,80,128]{2,1,0:T(8,128)(2,1)}), s16[16,80,128]{2,1,0:T(8,128)(2,1)S(1)}, u32[]{:S(2)}, u32[]{:S(2)}) async-start(s16[16,80,128]{2,1,0:T(8,128)(2,1)} %fit_and_gram.1), calls=%async_computation.1 | async-start | bytes 655360 | tf_op jit(solution)/shard_map/all_to_all | solution.py:201
  65.0 1.2 %collective-permute-start = (s16[1,80,128]{2,1,0:T(8,128)(2,1)S(1)}, s16[1,80,128]{2,1,0:T(8,128)(2,1)S(1)}, u32[]{:S(2)}, u32[]{:S(2)}) collective-permute-start(s16[1,80,128]{2,1,0:T(8,128)(2,1)S(1)} %constant_dynamic-slice_fusion), channel_id=1, source_target_pairs={{0,1},{1,0},{2,3},{3,2},{4,5},{5,4},{6,7},{7,6},{8,9},{9,8},{10,11... | collective-permute-start | bytes 61448 | tf_op jit(solution)/shard_map/ppermute | solution.py:204

commit v3 on v2

--- a/solution.py
+++ b/solution.py
@@ -9,28 +9,31 @@
 
 ROWS = 8
 LEVELS = 32000.0
+WINDOW = 4
+PATTERN = "FFFNFNFNFNNFNNF"
 PARTS = 4
 STEPS = 128.0
 FAST = pltpu.CompilerParams(vmem_limit_bytes=48 * 1024 * 1024)
 
 
-def half_kernel(
-    locality, screen, integrals, orbitals, half, taken, factors, places, flags, owner, sems
-):
-    tiles, reach, tile, _ = taken.shape
+def half_kernel(crossing, locality, screen, integrals, orbitals, *rest):
+    *halves, taken, factors, places, flags, owner, sems = rest
+    halves = halves[-taken.shape[0] :]
+    count, reach, tile, _ = taken.shape
+    tiles = 2 * count
+    me = lax.axis_index("aux")
+    order = [me ^ (count * crossing + k) for k in range(count)]
     total = tiles * lax.axis_size("bas")
     first = lax.axis_index("bas") * tiles
-    part = max(tiles // PARTS, 1)
+    part = max(count // PARTS, 1)
     small = [
         pltpu.make_async_copy(locality, places, sems.at[0]),
         pltpu.make_async_copy(screen, flags, sems.at[1]),
         pltpu.make_async_copy(orbitals, factors, sems.at[2]),
     ]
     blocks = [
-        pltpu.make_async_copy(
-            integrals.at[0, pl.ds(start, part)], taken.at[pl.ds(start, part)], sems.at[3 + k]
-        )
-        for k, start in enumerate(range(0, tiles, part))
+        pltpu.make_async_copy(integrals.at[0, centre], taken.at[k], sems.at[3 + k])
+        for k, centre in enumerate(order)
     ]
     for copy in small + blocks:
         copy.start()
@@ -39,24 +42,27 @@
         owner[places[j]] = j
     small[1].wait()
     small[2].wait()
-    for k, copy in enumerate(blocks):
-        copy.wait()
-        for c in range(k * part, (k + 1) * part):
-            j = owner[c]
-            product = jnp.dot(
-                taken[c].reshape(reach * tile, tile),
-                factors[j],
-                preferred_element_type=jnp.float32,
-            )
-            for d in range(reach):
-                block = first + c + d - reach // 2
-                inside = (block >= 0) & (block < total)
-                keep = jnp.where(inside, flags[d, 0, j], 0).astype(jnp.float32)
-                half[c, d] = (product[d * tile : (d + 1) * tile] * keep).astype(jnp.bfloat16)
-
-
-def gram_kernel(metric, rows, coded, fitted):
-    aux, reach, tile, _ = rows.shape
+    for k, centre in enumerate(order):
+        if k % part == 0:
+            for copy in blocks[k : k + part]:
+                copy.wait()
+        j = owner[centre]
+        product = jnp.dot(
+            taken[k].reshape(reach * tile, tile), factors[j], preferred_element_type=jnp.float32
+        )
+        for d in range(reach):
+            block = first + centre + d - reach // 2
+            inside = (block >= 0) & (block < total)
+            keep = jnp.where(inside, flags[d, 0, j], 0).astype(jnp.float32)
+            kept = (product[d * tile : (d + 1) * tile] * keep).astype(jnp.bfloat16)
+            halves[k][d] = kept
+
+
+def gram_kernel(metric, *rest):
+    *pieces, coded, fitted = rest
+    aux = len(pieces)
+    reach, tile, _ = pieces[0].shape
+    me = lax.axis_index("aux")
     group = 16
     wide = aux * group
     spread = (
@@ -64,8 +70,10 @@
         == lax.broadcasted_iota(jnp.int32, (wide, aux), 1)
     ).astype(jnp.bfloat16)
     picked = jnp.dot(spread, metric[...], preferred_element_type=jnp.float32).astype(jnp.bfloat16)
+    slot = lax.broadcasted_iota(jnp.int32, (wide, aux), 0) // group
+    from_slot = ((me ^ slot) == lax.broadcasted_iota(jnp.int32, (wide, aux), 1)).astype(jnp.bfloat16)
     mixer = lax.dot_general(
-        picked, spread, (((1,), (1,)), ((), ())), preferred_element_type=jnp.float32
+        picked, from_slot, (((1,), (1,)), ((), ())), preferred_element_type=jnp.float32
     )
     same_row = (
         lax.broadcasted_iota(jnp.int32, (wide, wide), 0) % group
@@ -74,10 +82,10 @@
     mixer = jnp.where(same_row, mixer, 0.0).astype(jnp.bfloat16)
     for d in range(reach):
         for g in range(0, tile, 2 * group):
-            pair = [
-                rows[:, d, g + s * group : g + (s + 1) * group, :].reshape(wide, tile)
-                for s in range(2)
-            ]
+            pair = []
+            for start in (g, g + group):
+                here = slice(start, start + group)
+                pair.append(jnp.concatenate([piece[d, here, :] for piece in pieces], axis=0))
             mixed = jnp.dot(
                 mixer, jnp.concatenate(pair, axis=1), preferred_element_type=jnp.float32
             ).astype(jnp.bfloat16)
@@ -163,41 +171,61 @@
 def body(integrals, orbitals, locality, screen, metric):
     _, tiles, reach, tile, _ = integrals.shape
     aux = lax.axis_size("aux")
-    if lax.axis_size("bas") != 2 or tiles != aux or reach != 3:
+    if lax.axis_size("bas") != 2 or tiles != aux or aux & (aux - 1) or reach != 3:
         raise ValueError("unsupported sizes")
     main_memory = pl.BlockSpec(memory_space=pltpu.HBM)
     vectors = pl.BlockSpec(memory_space=pltpu.VMEM)
-    half = pl.pallas_call(
-        half_kernel,
-        out_shape=jax.ShapeDtypeStruct((tiles, reach, tile, tile), jnp.bfloat16),
-        in_specs=[main_memory] * 4,
-        out_specs=vectors,
-        scratch_shapes=[
-            pltpu.VMEM((tiles, reach, tile, tile), jnp.bfloat16),
-            pltpu.VMEM((tiles, tile, tile), jnp.bfloat16),
-            pltpu.SMEM((tiles,), jnp.int32),
-            pltpu.SMEM((reach, 1, tiles), jnp.int32),
-            pltpu.SMEM((tiles,), jnp.int32),
-            pltpu.SemaphoreType.DMA((3 + PARTS,)),
-        ],
-        compiler_params=FAST,
-        name="half_transform",
-    )(*(
+    half = aux // 2
+    inputs = [
         pltpu.with_memory_space_constraint(array, pltpu.HBM)
         for array in (locality, jnp.transpose(screen, (2, 0, 1)), integrals, orbitals)
-    ))
-    rows = lax.all_to_all(half, "aux", split_axis=0, concat_axis=0, tiled=True)
+    ]
+    scratch = [
+        pltpu.VMEM((half, reach, tile, tile), jnp.bfloat16),
+        pltpu.VMEM((tiles, tile, tile), jnp.bfloat16),
+        pltpu.SMEM((tiles,), jnp.int32),
+        pltpu.SMEM((reach, 1, tiles), jnp.int32),
+        pltpu.SMEM((tiles,), jnp.int32),
+        pltpu.SemaphoreType.DMA((3 + half,)),
+    ]
+    far = pl.pallas_call(
+        functools.partial(half_kernel, True),
+        out_shape=[jax.ShapeDtypeStruct((reach, tile, tile), jnp.bfloat16)] * half,
+        in_specs=[main_memory] * 4,
+        out_specs=[vectors] * half,
+        scratch_shapes=scratch,
+        compiler_params=FAST,
+        name="half_far",
+    )(*inputs)
+    near = pl.pallas_call(
+        functools.partial(half_kernel, False),
+        out_shape=[jax.ShapeDtypeStruct((reach, tile, tile), jnp.bfloat16)] * half,
+        in_specs=[main_memory] * 4 + [pl.BlockSpec(memory_space=pl.ANY)],
+        out_specs=[vectors] * half,
+        scratch_shapes=scratch,
+        compiler_params=FAST,
+        name="half_near",
+    )(*inputs, far[0])
+    pieces = near + far
+    moved = {0: pieces[0]}
+    order = exchange_order(aux)
+    for t, k in enumerate(order):
+        piece = pieces[k]
+        if t >= WINDOW:
+            piece, _ = lax.optimization_barrier((piece, moved[order[t - WINDOW]]))
+        moved[k] = lax.ppermute(piece, "aux", [(i, i ^ k) for i in range(aux)])
+    pieces = [moved[k] for k in range(aux)]
     coded = pl.pallas_call(
         gram_kernel,
         out_shape=jax.ShapeDtypeStruct((aux, (reach * reach + 1) * ROWS, tile), jnp.int16),
-        in_specs=[vectors, vectors],
+        in_specs=[vectors] * (aux + 1),
         out_specs=vectors,
         scratch_shapes=[
             pltpu.VMEM((reach * tile, aux * tile), jnp.bfloat16),
         ],
         compiler_params=FAST,
         name="fit_and_gram",
-    )(metric, rows)
+    )(metric, *pieces)
     received = lax.all_to_all(coded, "aux", split_axis=0, concat_axis=0, tiled=True)
     edge = jnp.where(lax.axis_index("bas") == 0, tiles - 1, 0)
     edge_tile = lax.dynamic_slice_in_dim(received, edge, 1, 0)
@@ -215,6 +243,14 @@
     return jnp.transpose(band, (1, 0, 2))
 
 
+def exchange_order(devices):
+    half = devices // 2
+    far = [half + i // 2 + i % 2 * (half // 2) for i in range(half)]
+    near = list(range(half - 1, 0, -1))
+    turns = PATTERN if len(PATTERN) == devices - 1 else "F" + "FN" * (half - 1)
+    return [far.pop(0) if turn == "F" else near.pop(0) for turn in turns]
+
+
 def solution(mesh):
     placed = (
         P("aux", "bas", None, None, None),

time: 67.5 us -> 64.7 us (0.959)
  blocking collectives: 45.7 us -> 0 us
  starting transfers between devices: 3.89 us -> 31.4 us
  waiting for transfers between devices: 11.7 us -> 25.4 us
  Pallas kernels: 5.86 us -> 7.62 us
    all_to_all x1 -> x0, blocking collectives: 45.7 us -> none  [body(): rows = lax.all_to_all(half, 'aux', split_axis=0, concat_axis=0, tiled=True)]
    ppermute x0 -> x15, starting transfers between devices: none -> 27.9 us  [body(): moved[k] = lax.ppermute(piece, 'aux', [(i, i ^ k) for i in range(aux)])]
    ppermute x0 -> x15, waiting for transfers between devices: none -> 15.3 us  [body(): moved[k] = lax.ppermute(piece, 'aux', [(i, i ^ k) for i in range(aux)])]
    pallas_call x1 -> x2, Pallas kernels: 2.24 us -> 3.98 us  [the longest x1 1.99 us: body(): pl.pallas_call(functools.partial(half_kernel, False), out_shape=[jax.Shap...]
    all_to_all x1, waiting for transfers between devices: 10.5 us -> 8.96 us  [body(): lax.all_to_all(coded, 'aux', split_axis=0, concat_axis=0, tiled=True)]
  transfers between devices with their start and end apart: 2 -> 17, of which waited for: 2 -> 10; matrix products, arithmetic and copies ran while one was open for 0% -> 0% of each run, Pallas kernels for 0% -> 3%
where the time goes in v3:
time: 64.7 us; the launch traced here: 64.5 us
  starting transfers between devices  31.4 us (49%)
  waiting for transfers between devices  25.4 us (39%)
  Pallas kernels  7.62 us (12%)
    ppermute x15, starting transfers between devices, body(): moved[k] = lax.ppermute(piece, 'aux', [(i, i ^ k) for i in range(aux)])  27.9 us
    ppermute x15, waiting for transfers between devices, body(): moved[k] = lax.ppermute(piece, 'aux', [(i, i ^ k) for i in range(aux)])  15.3 us
    all_to_all x1, waiting for transfers between devices, body(): lax.all_to_all(coded, 'aux', split_axis=0, concat_axis=0, tiled=True)  8.96 us
    all_to_all x1, starting transfers between devices, body(): lax.all_to_all(coded, 'aux', split_axis=0, concat_axis=0, tiled=True)  3.54 us
    pallas_call x1, Pallas kernels, body(): pl.pallas_call(gram_kernel, out_shape=jax.ShapeDtypeStruct((aux, (reach *...  2.57 us
    pallas_call x1, Pallas kernels, body(): pl.pallas_call(functools.partial(half_kernel, False), out_shape=[jax.Shap...  1.99 us
    pallas_call x1, Pallas kernels, body(): pl.pallas_call(functools.partial(half_kernel, True), out_shape=[jax.Shape...  1.99 us
  transfers between devices with their start and end apart: 17, of which 10 were waited for; matrix products, arithmetic and copies ran while one was open for 0% of the time, Pallas kernels for 3%

profile of v3, /device:TPU:0, one launch (start us, length us, event | category | flops | bytes accessed | tf_op | source)
XLA Modules:
  0.0 64.5 jit_solution(2421241590035268157)
XLA Ops:
  0.0 2.0 %half_far.1 = (bf16[3,128,128]{2,1,0:T(8,128)(2,1)S(1)}, bf16[3,128,128]{2,1,0:T(8,128)(2,1)S(1)}, bf16[3,128,128]{2,1,0:T(8,128)(2,1)S(1)}, bf16[3,128,128]{2,1...) custom-call(s32[16]{0:T(128)} %locality.3, ...), custom_call_target="tpu_custom_call" | custom-call | tf_op jit(solution)/shard_map/half_far/pallas_call | solution.py:191
  2.0 0.0 copy-start
  2.0 5.1 %collective-permute-start = (bf16[3,128,128]{2,1,0:T(8,128)(2,1)S(1)}, bf16[3,128,128]{2,1,0:T(8,128)(2,1)S(1)}, u32[]{:S(2)}, u32[]{:S(2)}) collective-permute-start(bf16[3,128,128]{2,1,0:T(8,128)(2,1)S(1)} %get-tuple-element.37), channel_id=1, source_target_pairs={{0,24},{2,26},{4,28},{6,30},{8,16},{10,18},{12,20},{14,22},{16,8},... | collective-permute-start | bytes 294920 | tf_op jit(solution)/shard_map/ppermute | solution.py:216
  7.1 3.8 %collective-permute-start.8 = (bf16[3,128,128]{2,1,0:T(8,128)(2,1)S(1)}, bf16[3,128,128]{2,1,0:T(8,128)(2,1)S(1)}, u32[]{:S(2)}, u32[]{:S(2)}) collective-permute-start(bf16[3,128,128]{2,1,0:T(8,128)(2,1)S(1)} %get-tuple-element.49), channel_id=1, source_target_pairs={{0,18},{2,16},{4,22},{6,20},{8,26},{10,24},{12,30},{14,28},{16,2},... | collective-permute-start | bytes 294920 | tf_op jit(solution)/shard_map/ppermute | solution.py:216
  11.0 2.0 %half_near.1 = (bf16[3,128,128]{2,1,0:T(8,128)(2,1)S(1)}, bf16[3,128,128]{2,1,0:T(8,128)(2,1)S(1)}, bf16[3,128,128]{2,1,0:T(8,128)(2,1)S(1)}, bf16[3,128,128]{2,...) custom-call(s32[16]{0:T(128)} %locality.3, ...), custom_call_target="tpu_custom_call" | custom-call | tf_op jit(solution)/shard_map/half_near/pallas_call | solution.py:200
  13.0 0.5 collective-permute-start.11
  13.5 4.4 %collective-permute-start.1 = (bf16[3,128,128]{2,1,0:T(8,128)(2,1)S(1)}, bf16[3,128,128]{2,1,0:T(8,128)(2,1)S(1)}, u32[]{:S(2)}, u32[]{:S(2)}) collective-permute-start(bf16[3,128,128]{2,1,0:T(8,128)(2,1)S(1)} %get-tuple-element.38), channel_id=1, source_target_pairs={{0,12},{2,14},{4,8},{6,10},{8,4},{10,6},{12,0},{14,2},{16,28},{18,... | collective-permute-start | bytes 294920 | tf_op jit(solution)/shard_map/ppermute | solution.py:216
  17.9 0.7 %collective-permute-done.4.rest_8_ = bf16[3,128,128]{2,1,0:T(8,128)(2,1)S(1)} collective-permute-done((bf16[3,128,128]{2,1,0:T(8,128)(2,1)S(1)}, bf16[3,128,128]{2,1,0:T(8,128)(2,1)S(1)}, u32[]{:S(2)}, u32[]{:S(2)}) %collective-permute-start.4) | collective-permute-done | bytes 98336 | tf_op jit(solution)/shard_map/ppermute | solution.py:216
  18.6 3.5 %collective-permute-start.5 = (bf16[3,128,128]{2,1,0:T(8,128)(2,1)S(1)}, bf16[3,128,128]{2,1,0:T(8,128)(2,1)S(1)}, u32[]{:S(2)}, u32[]{:S(2)}) collective-permute-start(bf16[3,128,128]{2,1,0:T(8,128)(2,1)S(1)} %get-tuple-element.44), channel_id=1, source_target_pairs={{0,26},{2,24},{4,30},{6,28},{8,18},{10,16},{12,22},{14,20},{16,10}... | collective-permute-start | bytes 294920 | tf_op jit(solution)/shard_map/ppermute | solution.py:216
  22.1 0.0 collective-permute-done.8.rest_9_
  22.1 3.0 %collective-permute-done.11.rest_7_ = bf16[3,128,128]{2,1,0:T(8,128)(2,1)S(1)} collective-permute-done((bf16[3,128,128]{2,1,0:T(8,128)(2,1)S(1)}, bf16[3,128,128]{2,1,0:T(8,128)(2,1)S(1)}, u32[]{:S(2)}, u32[]{:S(2)}) %collective-permute-start.11) | collective-permute-done | bytes 98336 | tf_op jit(solution)/shard_map/ppermute | solution.py:216
  25.1 0.6 collective-permute-start.12
  25.6 0.0 collective-permute-done.1.rest_6_
  25.6 0.1 collective-permute-start.2
  25.7 0.5 collective-permute-done.5.rest_13_
  26.3 4.0 %collective-permute-start.6 = (bf16[3,128,128]{2,1,0:T(8,128)(2,1)S(1)}, bf16[3,128,128]{2,1,0:T(8,128)(2,1)S(1)}, u32[]{:S(2)}, u32[]{:S(2)}) collective-permute-start(bf16[3,128,128]{2,1,0:T(8,128)(2,1)S(1)} %get-tuple-element.45), channel_id=1, source_target_pairs={{0,28},{2,30},{4,24},{6,26},{8,20},{10,22},{12,16},{14,18},{16,12}... | collective-permute-start | bytes 294920 | tf_op jit(solution)/shard_map/ppermute | solution.py:216
  30.3 2.2 %collective-permute-done.9.rest_10_ = bf16[3,128,128]{2,1,0:T(8,128)(2,1)S(1)} collective-permute-done((bf16[3,128,128]{2,1,0:T(8,128)(2,1)S(1)}, bf16[3,128,128]{2,1,0:T(8,128)(2,1)S(1)}, u32[]{:S(2)}, u32[]{:S(2)}) %collective-permute-start.9) | collective-permute-done | bytes 98336 | tf_op jit(solution)/shard_map/ppermute | solution.py:216
  32.4 0.0 collective-permute-start.10
  32.5 0.3 collective-permute-done.12.rest_5_
  32.7 0.5 collective-permute-start.13
  33.3 0.0 collective-permute-done.2.rest_4_
  33.3 1.9 %collective-permute-start.3 = (bf16[3,128,128]{2,1,0:T(8,128)(2,1)S(1)}, bf16[3,128,128]{2,1,0:T(8,128)(2,1)S(1)}, u32[]{:S(2)}, u32[]{:S(2)}) collective-permute-start(bf16[3,128,128]{2,1,0:T(8,128)(2,1)S(1)} %get-tuple-element.40), channel_id=1, source_target_pairs={{0,2},{2,0},{4,6},{6,4},{8,10},{10,8},{12,14},{14,12},{16,18},{18,... | collective-permute-start | bytes 294920 | tf_op jit(solution)/shard_map/ppermute | solution.py:216
  35.2 1.6 %collective-permute-start.7 = (bf16[3,128,128]{2,1,0:T(8,128)(2,1)S(1)}, bf16[3,128,128]{2,1,0:T(8,128)(2,1)S(1)}, u32[]{:S(2)}, u32[]{:S(2)}) collective-permute-start(bf16[3,128,128]{2,1,0:T(8,128)(2,1)S(1)} %get-tuple-element.46), channel_id=1, source_target_pairs={{0,4},{2,6},{4,0},{6,2},{8,12},{10,14},{12,8},{14,10},{16,20},{18,... | collective-permute-start | bytes 294920 | tf_op jit(solution)/shard_map/ppermute | solution.py:216
  36.8 2.1 %collective-permute-done.10.rest_3_ = bf16[3,128,128]{2,1,0:T(8,128)(2,1)S(1)} collective-permute-done((bf16[3,128,128]{2,1,0:T(8,128)(2,1)S(1)}, bf16[3,128,128]{2,1,0:T(8,128)(2,1)S(1)}, u32[]{:S(2)}, u32[]{:S(2)}) %collective-permute-start.10) | collective-permute-done | bytes 98336 | tf_op jit(solution)/shard_map/ppermute | solution.py:216
  38.9 1.7 %collective-permute-start.14 = (bf16[3,128,128]{2,1,0:T(8,128)(2,1)S(1)}, bf16[3,128,128]{2,1,0:T(8,128)(2,1)S(1)}, u32[]{:S(2)}, u32[]{:S(2)}) collective-permute-start(bf16[3,128,128]{2,1,0:T(8,128)(2,1)S(1)} %get-tuple-element.58), channel_id=1, source_target_pairs={{0,30},{2,28},{4,26},{6,24},{8,22},{10,20},{12,18},{14,16},{16,14}... | collective-permute-start | bytes 294920 | tf_op jit(solution)/shard_map/ppermute | solution.py:216
  40.6 1.9 %collective-permute-done.13.rest_11_ = bf16[3,128,128]{2,1,0:T(8,128)(2,1)S(1)} collective-permute-done((bf16[3,128,128]{2,1,0:T(8,128)(2,1)S(1)}, bf16[3,128,128]{2,1,0:T(8,128)(2,1)S(1)}, u32[]{:S(2)}, u32[]{:S(2)}) %collective-permute-start.13) | collective-permute-done | bytes 98336 | tf_op jit(solution)/shard_map/ppermute | solution.py:216
  42.5 4.6 %collective-permute-done.14.rest_15_ = bf16[3,128,128]{2,1,0:T(8,128)(2,1)S(1)} collective-permute-done((bf16[3,128,128]{2,1,0:T(8,128)(2,1)S(1)}, bf16[3,128,128]{2,1,0:T(8,128)(2,1)S(1)}, u32[]{:S(2)}, u32[]{:S(2)}) %collective-permute-start.14) | collective-permute-done | bytes 98336 | tf_op jit(solution)/shard_map/ppermute | solution.py:216
  47.1 2.6 %fit_and_gram.1 = s16[16,80,128]{2,1,0:T(8,128)(2,1)} custom-call(bf16[16,16]{1,0:T(8,128)(2,1)S(1)} %copy-done, bf16[3,128,128]{2,1,0:T(8,128)(2,1)S(1)} %get-tuple-element.33.rest_0_, bf16[3,128,128]{2,1,0:T(8,128)(2,1)S(1)} %collective-permute-done.3.rest_1_, bf16[3,128,128]{2,1,0:T(8,128)(2,1)S(1)} %collective-permute-done.7.rest_2_, ...), custom_call_target="tpu_custom_call" | custom-call | tf_op jit(solution)/shard_map/fit_and_gram/pallas_call | solution.py:218
  49.7 3.5 %all-to-all-start = ((s16[16,80,128]{2,1,0:T(8,128)(2,1)}), s16[16,80,128]{2,1,0:T(8,128)(2,1)S(1)}, u32[]{:S(2)}, u32[]{:S(2)}) async-start(s16[16,80,128]{2,1,0:T(8,128)(2,1)} %fit_and_gram.1), calls=%async_computation | async-start | bytes 655360 | tf_op jit(solution)/shard_map/all_to_all | solution.py:229
  53.3 9.0 %all-to-all-done.received = s16[16,80,128]{2,1,0:T(8,128)(2,1)S(1)} async-done(((s16[16,80,128]{2,1,0:T(8,128)(2,1)}), s16[16,80,128]{2,1,0:T(8,128)(2,1)S(1)}, u32[]{:S(2)}, u32[]{:S(2)}) %all-to-all-start) | async-done | bytes 327712 | tf_op jit(solution)/shard_map/all_to_all | solution.py:229
  62.2 1.2 %collective-permute-done.15.rim = s16[1,80,128]{2,1,0:T(8,128)(2,1)S(1)} collective-permute-done((s16[1,80,128]{2,1,0:T(8,128)(2,1)S(1)}, s16[1,80,128]{2,1,0:T(8,128)(2,1)S(1)}, u32[]{:S(2)}, u32[]{:S(2)}) %collective-permute-start.15) | collective-permute-done | bytes 20512 | tf_op jit(solution)/shard_map/ppermute | solution.py:232
  63.4 1.1 %band_sum.1 = f32[5,16,1024]{2,1,0:T(8,128)} custom-call(s16[16,80,128]{2,1,0:T(8,128)(2,1)S(1)} %all-to-all-done.received, s16[1,80,128]{2,1,0:T(8,128)(2,1)S(1)} %collective-permute-done.15.rim), custom_call_target="tpu_custom_call" | custom-call | tf_op jit(solution)/shard_map/band_sum/pallas_call | solution.py:233
  (9 shorter events, 0.0 us)
Async XLA Ops:
  2.0 45.1 %copy-start = (bf16[16,16]{1,0:T(8,128)(2,1)S(1)}, bf16[16,16]{1,0:T(8,128)(2,1)}, u32[]{:S(2)}) copy-start(bf16[16,16]{1,0:T(8,128)(2,1)} %metric.1) | copy-start | bytes 1540
  2.0 11.5 %collective-permute-start = (bf16[3,128,128]{2,1,0:T(8,128)(2,1)S(1)}, bf16[3,128,128]{2,1,0:T(8,128)(2,1)S(1)}, u32[]{:S(2)}, u32[]{:S(2)}) collective-permute-start(bf16[3,128,128]{2,1,0:T(8,128)(2,1)S(1)} %get-tuple-element.37), channel_id=1, source_target_pairs={{0,24},{2,26},{4,28},{6,30},{8,16},{10,18},{12,20},{14,22},{16,8},... | collective-permute-start | bytes 294920 | tf_op jit(solution)/shard_map/ppermute | solution.py:216
  7.1 11.4 %collective-permute-start.4 = (bf16[3,128,128]{2,1,0:T(8,128)(2,1)S(1)}, bf16[3,128,128]{2,1,0:T(8,128)(2,1)S(1)}, u32[]{:S(2)}, u32[]{:S(2)}) collective-permute-start(bf16[3,128,128]{2,1,0:T(8,128)(2,1)S(1)} %get-tuple-element.32.rest_0_), channel_id=1, source_target_pairs={{0,16},{2,18},{4,20},{6,22},{8,24},{10,26},{12,28},{14,30},{16,0},... | collective-permute-start | bytes 294920 | tf_op jit(solution)/shard_map/ppermute | solution.py:216
  7.1 15.0 %collective-permute-start.8 = (bf16[3,128,128]{2,1,0:T(8,128)(2,1)S(1)}, bf16[3,128,128]{2,1,0:T(8,128)(2,1)S(1)}, u32[]{:S(2)}, u32[]{:S(2)}) collective-permute-start(bf16[3,128,128]{2,1,0:T(8,128)(2,1)S(1)} %get-tuple-element.49), channel_id=1, source_target_pairs={{0,18},{2,16},{4,22},{6,20},{8,26},{10,24},{12,30},{14,28},{16,2},... | collective-permute-start | bytes 294920 | tf_op jit(solution)/shard_map/ppermute | solution.py:216
  13.0 12.1 %collective-permute-start.11 = (bf16[3,128,128]{2,1,0:T(8,128)(2,1)S(1)}, bf16[3,128,128]{2,1,0:T(8,128)(2,1)S(1)}, u32[]{:S(2)}, u32[]{:S(2)}) collective-permute-start(bf16[3,128,128]{2,1,0:T(8,128)(2,1)S(1)} %get-tuple-element.53), channel_id=1, source_target_pairs={{0,14},{2,12},{4,10},{6,8},{8,6},{10,4},{12,2},{14,0},{16,30},{18,... | collective-permute-start | bytes 294920 | tf_op jit(solution)/shard_map/ppermute | solution.py:216
  13.5 12.1 %collective-permute-start.1 = (bf16[3,128,128]{2,1,0:T(8,128)(2,1)S(1)}, bf16[3,128,128]{2,1,0:T(8,128)(2,1)S(1)}, u32[]{:S(2)}, u32[]{:S(2)}) collective-permute-start(bf16[3,128,128]{2,1,0:T(8,128)(2,1)S(1)} %get-tuple-element.38), channel_id=1, source_target_pairs={{0,12},{2,14},{4,8},{6,10},{8,4},{10,6},{12,0},{14,2},{16,28},{18,... | collective-permute-start | bytes 294920 | tf_op jit(solution)/shard_map/ppermute | solution.py:216
  18.6 7.7 %collective-permute-start.5 = (bf16[3,128,128]{2,1,0:T(8,128)(2,1)S(1)}, bf16[3,128,128]{2,1,0:T(8,128)(2,1)S(1)}, u32[]{:S(2)}, u32[]{:S(2)}) collective-permute-start(bf16[3,128,128]{2,1,0:T(8,128)(2,1)S(1)} %get-tuple-element.44), channel_id=1, source_target_pairs={{0,26},{2,24},{4,30},{6,28},{8,18},{10,16},{12,22},{14,20},{16,10}... | collective-permute-start | bytes 294920 | tf_op jit(solution)/shard_map/ppermute | solution.py:216
  22.1 10.3 %collective-permute-start.9 = (bf16[3,128,128]{2,1,0:T(8,128)(2,1)S(1)}, bf16[3,128,128]{2,1,0:T(8,128)(2,1)S(1)}, u32[]{:S(2)}, u32[]{:S(2)}) collective-permute-start(bf16[3,128,128]{2,1,0:T(8,128)(2,1)S(1)} %get-tuple-element.50), channel_id=1, source_target_pairs={{0,20},{2,22},{4,16},{6,18},{8,28},{10,30},{12,24},{14,26},{16,4},... | collective-permute-start | bytes 294920 | tf_op jit(solution)/shard_map/ppermute | solution.py:216
  25.1 7.7 %collective-permute-start.12 = (bf16[3,128,128]{2,1,0:T(8,128)(2,1)S(1)}, bf16[3,128,128]{2,1,0:T(8,128)(2,1)S(1)}, u32[]{:S(2)}, u32[]{:S(2)}) collective-permute-start(bf16[3,128,128]{2,1,0:T(8,128)(2,1)S(1)} %get-tuple-element.54), channel_id=1, source_target_pairs={{0,10},{2,8},{4,14},{6,12},{8,2},{10,0},{12,6},{14,4},{16,26},{18,... | collective-permute-start | bytes 294920 | tf_op jit(solution)/shard_map/ppermute | solution.py:216
  25.6 7.6 %collective-permute-start.2 = (bf16[3,128,128]{2,1,0:T(8,128)(2,1)S(1)}, bf16[3,128,128]{2,1,0:T(8,128)(2,1)S(1)}, u32[]{:S(2)}, u32[]{:S(2)}) collective-permute-start(bf16[3,128,128]{2,1,0:T(8,128)(2,1)S(1)} %get-tuple-element.39), channel_id=1, source_target_pairs={{0,8},{2,10},{4,12},{6,14},{8,0},{10,2},{12,4},{14,6},{16,24},{18,... | collective-permute-start | bytes 294920 | tf_op jit(solution)/shard_map/ppermute | solution.py:216
  26.3 9.0 %collective-permute-start.6 = (bf16[3,128,128]{2,1,0:T(8,128)(2,1)S(1)}, bf16[3,128,128]{2,1,0:T(8,128)(2,1)S(1)}, u32[]{:S(2)}, u32[]{:S(2)}) collective-permute-start(bf16[3,128,128]{2,1,0:T(8,128)(2,1)S(1)} %get-tuple-element.45), channel_id=1, source_target_pairs={{0,28},{2,30},{4,24},{6,26},{8,20},{10,22},{12,16},{14,18},{16,12}... | collective-permute-start | bytes 294920 | tf_op jit(solution)/shard_map/ppermute | solution.py:216
  32.4 6.5 %collective-permute-start.10 = (bf16[3,128,128]{2,1,0:T(8,128)(2,1)S(1)}, bf16[3,128,128]{2,1,0:T(8,128)(2,1)S(1)}, u32[]{:S(2)}, u32[]{:S(2)}) collective-permute-start(bf16[3,128,128]{2,1,0:T(8,128)(2,1)S(1)} %get-tuple-element.51), channel_id=1, source_target_pairs={{0,6},{2,4},{4,2},{6,0},{8,14},{10,12},{12,10},{14,8},{16,22},{18,... | collective-permute-start | bytes 294920 | tf_op jit(solution)/shard_map/ppermute | solution.py:216
  32.7 9.8 %collective-permute-start.13 = (bf16[3,128,128]{2,1,0:T(8,128)(2,1)S(1)}, bf16[3,128,128]{2,1,0:T(8,128)(2,1)S(1)}, u32[]{:S(2)}, u32[]{:S(2)}) collective-permute-start(bf16[3,128,128]{2,1,0:T(8,128)(2,1)S(1)} %get-tuple-element.56), channel_id=1, source_target_pairs={{0,22},{2,20},{4,18},{6,16},{8,30},{10,28},{12,26},{14,24},{16,6},... | collective-permute-start | bytes 294920 | tf_op jit(solution)/shard_map/ppermute | solution.py:216
  33.3 9.3 %collective-permute-start.3 = (bf16[3,128,128]{2,1,0:T(8,128)(2,1)S(1)}, bf16[3,128,128]{2,1,0:T(8,128)(2,1)S(1)}, u32[]{:S(2)}, u32[]{:S(2)}) collective-permute-start(bf16[3,128,128]{2,1,0:T(8,128)(2,1)S(1)} %get-tuple-element.40), channel_id=1, source_target_pairs={{0,2},{2,0},{4,6},{6,4},{8,10},{10,8},{12,14},{14,12},{16,18},{18,... | collective-permute-start | bytes 294920 | tf_op jit(solution)/shard_map/ppermute | solution.py:216
  35.2 7.3 %collective-permute-start.7 = (bf16[3,128,128]{2,1,0:T(8,128)(2,1)S(1)}, bf16[3,128,128]{2,1,0:T(8,128)(2,1)S(1)}, u32[]{:S(2)}, u32[]{:S(2)}) collective-permute-start(bf16[3,128,128]{2,1,0:T(8,128)(2,1)S(1)} %get-tuple-element.46), channel_id=1, source_target_pairs={{0,4},{2,6},{4,0},{6,2},{8,12},{10,14},{12,8},{14,10},{16,20},{18,... | collective-permute-start | bytes 294920 | tf_op jit(solution)/shard_map/ppermute | solution.py:216
  38.9 8.2 %collective-permute-start.14 = (bf16[3,128,128]{2,1,0:T(8,128)(2,1)S(1)}, bf16[3,128,128]{2,1,0:T(8,128)(2,1)S(1)}, u32[]{:S(2)}, u32[]{:S(2)}) collective-permute-start(bf16[3,128,128]{2,1,0:T(8,128)(2,1)S(1)} %get-tuple-element.58), channel_id=1, source_target_pairs={{0,30},{2,28},{4,26},{6,24},{8,22},{10,20},{12,18},{14,16},{16,14}... | collective-permute-start | bytes 294920 | tf_op jit(solution)/shard_map/ppermute | solution.py:216
  49.7 12.5 %all-to-all-start = ((s16[16,80,128]{2,1,0:T(8,128)(2,1)}), s16[16,80,128]{2,1,0:T(8,128)(2,1)S(1)}, u32[]{:S(2)}, u32[]{:S(2)}) async-start(s16[16,80,128]{2,1,0:T(8,128)(2,1)} %fit_and_gram.1), calls=%async_computation | async-start | bytes 655360 | tf_op jit(solution)/shard_map/all_to_all | solution.py:229
  62.2 1.2 %collective-permute-start.15 = (s16[1,80,128]{2,1,0:T(8,128)(2,1)S(1)}, s16[1,80,128]{2,1,0:T(8,128)(2,1)S(1)}, u32[]{:S(2)}, u32[]{:S(2)}) collective-permute-start(s16[1,80,128]{2,1,0:T(8,128)(2,1)S(1)} %constant_dynamic-slice_fusion), channel_id=1, source_target_pairs={{0,1},{1,0},{2,3},{3,2},{4,5},{5,4},{6,7},{7,6},{8,9},{9,8},{10,11... | collective-permute-start | bytes 61448 | tf_op jit(solution)/shard_map/ppermute | solution.py:232

commit v4 on v3

v4 whole, which is shorter than its diff:
```python
import functools

import jax
import jax.numpy as jnp
from jax import lax
from jax.experimental import pallas as pl
from jax.experimental.pallas import tpu as pltpu
from jax.sharding import PartitionSpec as P

ROWS = 8
LEVELS = 32000.0
GROUP = 16
HEAD = 8
ORDERS = (
    [8, 13, 7, 6, 9, 5, 12, 4, 10, 3, 2, 14, 11, 1, 15],
    [10, 5, 11, 7, 15, 6, 8, 14, 12, 1, 3, 9, 2, 4, 13],
)
WINDOWS = [4] * 15
PARTS = 2
STEPS = 128.0
FAST = pltpu.CompilerParams(vmem_limit_bytes=48 * 1024 * 1024)


def exchange_orders(devices):
    if devices - 1 == len(ORDERS[0]):
        return ORDERS
    half = devices // 2
    order = [half]
    for k in range(1, half):
        order += [k, half + k]
    return order, order


def partner(t):
    first, second = exchange_orders(lax.axis_size("aux"))
    return jnp.where(lax.axis_index("bas") == 0, first[t], second[t])


def half_kernel(slots, locality, screen, integrals, orbitals, *rest):
    *halves, taken, factors, places, flags, owner, sems = rest
    if slots[-1] is None:
        metric, _, *halves, mixer = halves
    count, reach, tile, _ = taken.shape
    tiles = factors.shape[0]
    me = lax.axis_index("aux")
    order = [me if t is None else me ^ partner(t) for t in slots]
    total = tiles * lax.axis_size("bas")
    first = lax.axis_index("bas") * tiles
    part = max(count // PARTS, 1)
    small = [
        pltpu.make_async_copy(locality, places, sems.at[0]),
        pltpu.make_async_copy(screen, flags, sems.at[1]),
        pltpu.make_async_copy(orbitals, factors, sems.at[2]),
    ]
    blocks = [
        pltpu.make_async_copy(integrals.at[0, centre], taken.at[k], sems.at[3 + k])
        for k, centre in enumerate(order)
    ]
    for copy in small + blocks:
        copy.start()
    small[0].wait()
    for j in range(tiles):
        owner[places[j]] = j
    small[1].wait()
    small[2].wait()
    if slots[-1] is None:
        write_mixer(metric, mixer)
    for k, centre in enumerate(order):
        if k % part == 0:
            for copy in blocks[k : k + part]:
                copy.wait()
        j = owner[centre]
        product = jnp.dot(
            taken[k].reshape(reach * tile, tile), factors[j], preferred_element_type=jnp.float32
        )
        for d in range(reach):
            block = first + centre + d - reach // 2
            inside = (block >= 0) & (block < total)
            keep = jnp.where(inside, flags[d, 0, j], 0).astype(jnp.float32)
            kept = (product[d * tile : (d + 1) * tile] * keep).astype(jnp.bfloat16)
            halves[k][d] = kept


def write_mixer(metric, mixer):
    aux = metric.shape[0]
    wide = mixer.shape[0]
    group = wide // aux
    me = lax.axis_index("aux")
    slot = lax.broadcasted_iota(jnp.int32, (aux, aux), 0)
    came = jnp.full((aux, aux), me, jnp.int32)
    for t in range(aux - 1):
        came = jnp.where(slot == t + 1, me ^ partner(t), came)
    from_slot = (came == lax.broadcasted_iota(jnp.int32, (aux, aux), 1)).astype(jnp.bfloat16)
    placed = lax.dot_general(
        metric[...], from_slot, (((1,), (1,)), ((), ())), preferred_element_type=jnp.float32
    ).astype(jnp.bfloat16)
    spread = (
        lax.broadcasted_iota(jnp.int32, (wide, aux), 0) // group
        == lax.broadcasted_iota(jnp.int32, (wide, aux), 1)
    ).astype(jnp.bfloat16)
    picked = jnp.dot(spread, placed, preferred_element_type=jnp.float32).astype(jnp.bfloat16)
    full = lax.dot_general(
        picked, spread, (((1,), (1,)), ((), ())), preferred_element_type=jnp.float32
    )
    same_row = (
        lax.broadcasted_iota(jnp.int32, (wide, wide), 0) % group
        == lax.broadcasted_iota(jnp.int32, (wide, wide), 1) % group
    )
    mixer[...] = jnp.where(same_row, full, 0.0).astype(jnp.bfloat16)


def gram_kernel(mixer, *rest):
    *pieces, coded, fitted = rest
    aux = len(pieces)
    reach, tile, _ = pieces[0].shape
    group = GROUP
    wide = aux * group
    for d in range(reach):
        for g in range(0, tile, 2 * group):
            pair = []
            for start in (g, g + group):
                here = slice(start, start + group)
                pair.append(jnp.concatenate([piece[d, here, :] for piece in pieces], axis=0))
            mixed = jnp.dot(
                mixer[...], jnp.concatenate(pair, axis=1), preferred_element_type=jnp.float32
            ).astype(jnp.bfloat16)
            for s in range(2):
                start = d * tile + g + s * group
                for q in range(aux):
                    fitted[start : start + group, q * tile : (q + 1) * tile] = mixed[
                        q * group : (q + 1) * group, s * tile : (s + 1) * tile
                    ]
    gram = lax.dot_general(
        fitted[...], fitted[...], (((1,), (1,)), ((), ())), preferred_element_type=jnp.float32
    )
    lane = lax.broadcasted_iota(jnp.int32, (ROWS, tile), 1)
    owners = coded.shape[0]
    per = tile // owners
    for a in range(owners):
        codes, scales = [], jnp.zeros((ROWS, tile), jnp.float32)
        for d in range(reach):
            rows = gram[d * tile + a * per : d * tile + (a + 1) * per]
            if per < ROWS:
                rows = jnp.pad(rows, ((0, ROWS - per), (0, 0)))
            code, scale = encode(rows)
            codes += [code[:, d2 * tile : (d2 + 1) * tile] for d2 in range(reach)]
            scales = jnp.where(lane == d, scale, scales)
        sent = jnp.concatenate(codes + [scales], axis=0)
        coded[a] = sent.astype(jnp.int32).astype(jnp.int16)


def encode(rows):
    peak = jnp.max(jnp.abs(rows), axis=1, keepdims=True)
    scale = jnp.ceil(jnp.log2(jnp.maximum(peak, 1e-37)) * STEPS)
    return jnp.round(rows * jnp.exp2(scale * (-1.0 / STEPS)) * LEVELS), scale


def decode(sent, reach):
    sent = sent.astype(jnp.int32).astype(jnp.float32)
    scales = sent[reach * reach * ROWS :]
    blocks = []
    for d in range(reach):
        factor = jnp.exp2(scales[:, d : d + 1] * (1.0 / STEPS))
        starts = [(d * reach + d2) * ROWS for d2 in range(reach)]
        blocks.append([sent[i : i + ROWS] * (1.0 / LEVELS) * factor for i in starts])
    return blocks


def band_kernel(reach, received, band):
    centres, _, tile = received.shape
    per = band.shape[2] // tile
    offsets = 2 * reach - 1
    middle = reach // 2
    sums = {}

    def finish(m):
        for e in range(offsets):
            total = sums.pop((m, e), jnp.zeros((ROWS, tile), jnp.float32))
            for r in range(per):
                band[e, m : m + 1, r * tile : (r + 1) * tile] = total[r : r + 1]

    for c in range(centres):
        blocks = decode(received[c], reach)
        for d in range(reach):
            m = c + d - middle
            if 0 <= m < centres:
                for d2 in range(reach):
                    key = m, d2 - d + reach - 1
                    piece = blocks[d][d2]
                    sums[key] = sums[key] + piece if key in sums else piece
        if c >= middle:
            finish(c - middle)
    for m in range(centres - middle, centres):
        finish(m)


def rim_kernel(reach, part, rim, band):
    band[...] = part[...]
    tile = rim.shape[2]
    per = band.shape[2] // tile
    blocks = decode(rim[0], reach)

    def add(m, d, first):
        for d2 in range(reach):
            for r in range(per):
                here = first + d2, slice(m, m + 1), slice(r * tile, (r + 1) * tile)
                band[here] += blocks[d][d2][r : r + 1]

    @pl.when(lax.axis_index("bas") == 0)
    def _():
        add(band.shape[1] - 1, 0, reach - 1)

    @pl.when(lax.axis_index("bas") != 0)
    def _():
        add(0, reach - 1, 0)


def body(integrals, orbitals, locality, screen, metric):
    _, tiles, reach, tile, _ = integrals.shape
    aux = lax.axis_size("aux")
    if lax.axis_size("bas") != 2 or tiles != aux or aux & (aux - 1) or reach != 3:
        raise ValueError("unsupported sizes")
    main_memory = pl.BlockSpec(memory_space=pltpu.HBM)
    vectors = pl.BlockSpec(memory_space=pltpu.VMEM)
    inputs = [
        pltpu.with_memory_space_constraint(array, pltpu.HBM)
        for array in (locality, jnp.transpose(screen, (2, 0, 1)), integrals, orbitals)
    ]

    def half_rows(slots, more, out_shape, name):
        return pl.pallas_call(
            functools.partial(half_kernel, slots),
            out_shape=[jax.ShapeDtypeStruct((reach, tile, tile), jnp.bfloat16)] * len(slots)
            + out_shape,
            in_specs=[main_memory] * 4 + [vectors, pl.BlockSpec(memory_space=pl.ANY)][: len(more)],
            out_specs=[vectors] * (len(slots) + len(out_shape)),
            scratch_shapes=[
                pltpu.VMEM((len(slots), reach, tile, tile), jnp.bfloat16),
                pltpu.VMEM((tiles, tile, tile), jnp.bfloat16),
                pltpu.SMEM((tiles,), jnp.int32),
                pltpu.SMEM((reach, 1, tiles), jnp.int32),
                pltpu.SMEM((tiles,), jnp.int32),
                pltpu.SemaphoreType.DMA((3 + len(slots),)),
            ],
            compiler_params=FAST,
            name=name,
        )(*inputs, *more)

    head = min(HEAD, aux - 1)
    early = half_rows(list(range(head)), [], [], "half_early")
    *late, own, mixer = half_rows(
        list(range(head, aux - 1)) + [None],
        [metric, early[0]],
        [jax.ShapeDtypeStruct((aux * GROUP, aux * GROUP), jnp.bfloat16)],
        "half_late",
    )
    orders = exchange_orders(aux)
    windows = WINDOWS if len(WINDOWS) == aux - 1 else [4] * aux
    moved = []
    for t, piece in enumerate([*early, *late]):
        if t >= windows[t]:
            piece, _ = lax.optimization_barrier((piece, moved[t - windows[t]]))
        pairs = [
            (2 * i + core, 2 * (i ^ orders[core][t]) + core) for i in range(aux) for core in (0, 1)
        ]
        moved.append(lax.ppermute(piece, ("aux", "bas"), pairs))
    pieces = [own] + moved
    coded = pl.pallas_call(
        gram_kernel,
        out_shape=jax.ShapeDtypeStruct((aux, (reach * reach + 1) * ROWS, tile), jnp.int16),
        in_specs=[vectors] * (aux + 1),
        out_specs=vectors,
        scratch_shapes=[
            pltpu.VMEM((reach * tile, aux * tile), jnp.bfloat16),
        ],
        compiler_params=FAST,
        name="fit_and_gram",
    )(mixer, *pieces)
    received = lax.all_to_all(coded, "aux", split_axis=0, concat_axis=0, tiled=True)
    edge = jnp.where(lax.axis_index("bas") == 0, tiles - 1, 0)
    edge_tile = lax.dynamic_slice_in_dim(received, edge, 1, 0)
    rim = lax.ppermute(edge_tile, "bas", [(0, 1), (1, 0)])
    share = jax.ShapeDtypeStruct((2 * reach - 1, tiles, tile * tile // aux), jnp.float32)
    part = pl.pallas_call(
        functools.partial(band_kernel, reach),
        out_shape=share,
        in_specs=[vectors],
        out_specs=vectors,
        compiler_params=FAST,
        name="band_sum",
    )(received)
    band = pl.pallas_call(
        functools.partial(rim_kernel, reach),
        out_shape=share,
        in_specs=[vectors, vectors],
        out_specs=vectors,
        compiler_params=FAST,
        name="band_rim",
    )(part, rim)
    return jnp.transpose(band, (1, 0, 2))


def solution(mesh):
    placed = (
        P("aux", "bas", None, None, None),
        P("bas", None, None),
        P("bas"),
        P("aux", "bas", None),
        P(),
    )
    return jax.shard_map(
        body, mesh=mesh, in_specs=placed, out_specs=P("bas", None, "aux"), check_vma=False
    )
```

time: 64.7 us -> 61.4 us (0.949)
  waiting for transfers between devices: 25.4 us -> 21.4 us
  starting transfers between devices: 31.4 us -> 32.3 us
    ppermute x15, waiting for transfers between devices: 15.3 us -> 11.5 us  [body(): moved.append(lax.ppermute(piece, ('aux', 'bas'), pairs))]
    all_to_all x1, starting transfers between devices: 3.54 us -> 4.47 us  [body(): lax.all_to_all(coded, 'aux', split_axis=0, concat_axis=0, tiled=True)]
    pallas_call x3 -> x4, Pallas kernels: 5.05 us -> 5.01 us  [the longest x2 3.93 us: half_rows(): pl.pallas_call(functools.partial(half_kernel, slots), out_shape=[jax.Shap...]
  transfers between devices with their start and end apart: 17 -> 17, of which waited for: 10 -> 8; matrix products, arithmetic and copies ran while one was open for 0% -> 0% of each run, Pallas kernels for 3% -> 4%
where the time goes in v4:
time: 61.4 us; the launch traced here: 61.2 us
  starting transfers between devices  32.3 us (53%)
  waiting for transfers between devices  21.4 us (35%)
  Pallas kernels  7.39 us (12%)
    ppermute x15, starting transfers between devices, body(): moved.append(lax.ppermute(piece, ('aux', 'bas'), pairs))  27.8 us
    ppermute x15, waiting for transfers between devices, body(): moved.append(lax.ppermute(piece, ('aux', 'bas'), pairs))  11.5 us
    all_to_all x1, waiting for transfers between devices, body(): lax.all_to_all(coded, 'aux', split_axis=0, concat_axis=0, tiled=True)  9 us
    all_to_all x1, starting transfers between devices, body(): lax.all_to_all(coded, 'aux', split_axis=0, concat_axis=0, tiled=True)  4.47 us
    pallas_call x2, Pallas kernels, half_rows(): pl.pallas_call(functools.partial(half_kernel, slots), out_shape=[jax.Shap...  3.93 us
    pallas_call x1, Pallas kernels, body(): pl.pallas_call(gram_kernel, out_shape=jax.ShapeDtypeStruct((aux, (reach *...  2.38 us
  transfers between devices with their start and end apart: 17, of which 8 were waited for; matrix products, arithmetic and copies ran while one was open for 0% of the time, Pallas kernels for 4%

profile of v4, /device:TPU:0, one launch (start us, length us, event | category | flops | bytes accessed | tf_op | source)
XLA Modules:
  0.0 61.2 jit_solution(17688780283673626348)
XLA Ops:
  0.0 1.8 %half_early.1 = (bf16[3,128,128]{2,1,0:T(8,128)(2,1)S(1)}, bf16[3,128,128]{2,1,0:T(8,128)(2,1)S(1)}, bf16[3,128,128]{2,1,0:T(8,128)(2,1)S(1)}, bf16[3,128,128]{2...) custom-call(s32[16]{0:T(128)} %locality.3, ...), custom_call_target="tpu_custom_call" | custom-call | tf_op jit(solution)/shard_map/half_early/pallas_call | solution.py:231
  1.8 4.1 %collective-permute-start = (bf16[3,128,128]{2,1,0:T(8,128)(2,1)S(1)}, bf16[3,128,128]{2,1,0:T(8,128)(2,1)S(1)}, u32[]{:S(2)}, u32[]{:S(2)}) collective-permute-start(bf16[3,128,128]{2,1,0:T(8,128)(2,1)S(1)} %get-tuple-element.33.rest_1_), channel_id=1, source_target_pairs={{0,16},{1,21},{2,18},{3,23},{4,20},{5,17},{6,22},{7,19},{8,24},{9,... | collective-permute-start | bytes 294920 | tf_op jit(solution)/shard_map/ppermute | solution.py:266
  5.9 3.5 %collective-permute-start.2 = (bf16[3,128,128]{2,1,0:T(8,128)(2,1)S(1)}, bf16[3,128,128]{2,1,0:T(8,128)(2,1)S(1)}, u32[]{:S(2)}, u32[]{:S(2)}) collective-permute-start(bf16[3,128,128]{2,1,0:T(8,128)(2,1)S(1)} %get-tuple-element.37), channel_id=1, source_target_pairs={{0,14},{1,23},{2,12},{3,21},{4,10},{5,19},{6,8},{7,17},{8,6},{9,31... | collective-permute-start | bytes 294920 | tf_op jit(solution)/shard_map/ppermute | solution.py:266
  9.3 0.2 collective-permute-start.1
  9.5 0.6 %collective-permute-start.3 = (bf16[3,128,128]{2,1,0:T(8,128)(2,1)S(1)}, bf16[3,128,128]{2,1,0:T(8,128)(2,1)S(1)}, u32[]{:S(2)}, u32[]{:S(2)}) collective-permute-start(bf16[3,128,128]{2,1,0:T(8,128)(2,1)S(1)} %get-tuple-element.38), channel_id=1, source_target_pairs={{0,12},{1,15},{2,14},{3,13},{4,8},{5,11},{6,10},{7,9},{8,4},{9,7},... | collective-permute-start | bytes 294920 | tf_op jit(solution)/shard_map/ppermute | solution.py:266
  10.2 1.4 %collective-permute-done.rest_1_ = bf16[3,128,128]{2,1,0:T(8,128)(2,1)S(1)} collective-permute-done((bf16[3,128,128]{2,1,0:T(8,128)(2,1)S(1)}, bf16[3,128,128]{2,1,0:T(8,128)(2,1)S(1)}, u32[]{:S(2)}, u32[]{:S(2)}) %collective-permute-start) | collective-permute-done | bytes 98336 | tf_op jit(solution)/shard_map/ppermute | solution.py:266
  11.6 3.0 %collective-permute-start.4 = (bf16[3,128,128]{2,1,0:T(8,128)(2,1)S(1)}, bf16[3,128,128]{2,1,0:T(8,128)(2,1)S(1)}, u32[]{:S(2)}, u32[]{:S(2)}) collective-permute-start(bf16[3,128,128]{2,1,0:T(8,128)(2,1)S(1)} %get-tuple-element.40), channel_id=1, source_target_pairs={{0,18},{1,31},{2,16},{3,29},{4,22},{5,27},{6,20},{7,25},{8,26},{9,... | collective-permute-start | bytes 294920 | tf_op jit(solution)/shard_map/ppermute | solution.py:266
  14.6 0.0 collective-permute-done.2.rest_3_
  14.6 2.5 %collective-permute-start.6 = (bf16[3,128,128]{2,1,0:T(8,128)(2,1)S(1)}, bf16[3,128,128]{2,1,0:T(8,128)(2,1)S(1)}, u32[]{:S(2)}, u32[]{:S(2)}) collective-permute-start(bf16[3,128,128]{2,1,0:T(8,128)(2,1)S(1)} %get-tuple-element.44), channel_id=1, source_target_pairs={{0,24},{1,17},{2,26},{3,19},{4,28},{5,21},{6,30},{7,23},{8,16},{9,... | collective-permute-start | bytes 294920 | tf_op jit(solution)/shard_map/ppermute | solution.py:266
  17.1 0.2 collective-permute-done.1.rest_2_
  17.3 0.7 %collective-permute-start.5 = (bf16[3,128,128]{2,1,0:T(8,128)(2,1)S(1)}, bf16[3,128,128]{2,1,0:T(8,128)(2,1)S(1)}, u32[]{:S(2)}, u32[]{:S(2)}) collective-permute-start(bf16[3,128,128]{2,1,0:T(8,128)(2,1)S(1)} %get-tuple-element.42), channel_id=1, source_target_pairs={{0,10},{1,13},{2,8},{3,15},{4,14},{5,9},{6,12},{7,11},{8,2},{9,5},... | collective-permute-start | bytes 294920 | tf_op jit(solution)/shard_map/ppermute | solution.py:266
  18.0 2.2 %half_late.1 = (bf16[3,128,128]{2,1,0:T(8,128)(2,1)S(1)}, bf16[3,128,128]{2,1,0:T(8,128)(2,1)S(1)}, bf16[3,128,128]{2,1,0:T(8,128)(2,1)S(1)}, bf16[3,128,128]{2,...) custom-call(s32[16]{0:T(128)} %locality.3, ...), custom_call_target="tpu_custom_call" | custom-call | tf_op jit(solution)/shard_map/half_late/pallas_call | solution.py:231
  20.2 1.9 %collective-permute-start.7 = (bf16[3,128,128]{2,1,0:T(8,128)(2,1)S(1)}, bf16[3,128,128]{2,1,0:T(8,128)(2,1)S(1)}, u32[]{:S(2)}, u32[]{:S(2)}) collective-permute-start(bf16[3,128,128]{2,1,0:T(8,128)(2,1)S(1)} %get-tuple-element.46), channel_id=1, source_target_pairs={{0,8},{1,29},{2,10},{3,31},{4,12},{5,25},{6,14},{7,27},{8,0},{9,21... | collective-permute-start | bytes 294920 | tf_op jit(solution)/shard_map/ppermute | solution.py:266
  22.0 1.5 %collective-permute-done.4.rest_5_ = bf16[3,128,128]{2,1,0:T(8,128)(2,1)S(1)} collective-permute-done((bf16[3,128,128]{2,1,0:T(8,128)(2,1)S(1)}, bf16[3,128,128]{2,1,0:T(8,128)(2,1)S(1)}, u32[]{:S(2)}, u32[]{:S(2)}) %collective-permute-start.4) | collective-permute-done | bytes 98336 | tf_op jit(solution)/shard_map/ppermute | solution.py:266
  23.6 1.1 %collective-permute-start.8 = (bf16[3,128,128]{2,1,0:T(8,128)(2,1)S(1)}, bf16[3,128,128]{2,1,0:T(8,128)(2,1)S(1)}, u32[]{:S(2)}, u32[]{:S(2)}) collective-permute-start(bf16[3,128,128]{2,1,0:T(8,128)(2,1)S(1)} %get-tuple-element.48), channel_id=1, source_target_pairs={{0,20},{1,25},{2,22},{3,27},{4,16},{5,29},{6,18},{7,31},{8,28},{9,... | collective-permute-start | bytes 294920 | tf_op jit(solution)/shard_map/ppermute | solution.py:266
  24.7 0.0 collective-permute-done.6.rest_7_
  24.7 0.8 %collective-permute-start.10 = (bf16[3,128,128]{2,1,0:T(8,128)(2,1)S(1)}, bf16[3,128,128]{2,1,0:T(8,128)(2,1)S(1)}, u32[]{:S(2)}, u32[]{:S(2)}) collective-permute-start(bf16[3,128,128]{2,1,0:T(8,128)(2,1)S(1)} %get-tuple-element.52), channel_id=1, source_target_pairs={{0,4},{1,7},{2,6},{3,5},{4,0},{5,3},{6,2},{7,1},{8,12},{9,15},{10,... | collective-permute-start | bytes 294920 | tf_op jit(solution)/shard_map/ppermute | solution.py:266
  25.5 0.2 collective-permute-done.5.rest_6_
  25.6 1.8 %collective-permute-start.9 = (bf16[3,128,128]{2,1,0:T(8,128)(2,1)S(1)}, bf16[3,128,128]{2,1,0:T(8,128)(2,1)S(1)}, u32[]{:S(2)}, u32[]{:S(2)}) collective-permute-start(bf16[3,128,128]{2,1,0:T(8,128)(2,1)S(1)} %get-tuple-element.50), channel_id=1, source_target_pairs={{0,6},{1,3},{2,4},{3,1},{4,2},{5,7},{6,0},{7,5},{8,14},{9,11},{10,... | collective-permute-start | bytes 294920 | tf_op jit(solution)/shard_map/ppermute | solution.py:266
  27.4 0.0 collective-permute-done.7.rest_8_
  27.5 3.5 %collective-permute-start.11 = (bf16[3,128,128]{2,1,0:T(8,128)(2,1)S(1)}, bf16[3,128,128]{2,1,0:T(8,128)(2,1)S(1)}, u32[]{:S(2)}, u32[]{:S(2)}) collective-permute-start(bf16[3,128,128]{2,1,0:T(8,128)(2,1)S(1)} %get-tuple-element.54), channel_id=1, source_target_pairs={{0,28},{1,19},{2,30},{3,17},{4,24},{5,23},{6,26},{7,21},{8,20},{9,... | collective-permute-start | bytes 294920 | tf_op jit(solution)/shard_map/ppermute | solution.py:266
  30.9 2.5 %collective-permute-done.8.rest_9_ = bf16[3,128,128]{2,1,0:T(8,128)(2,1)S(1)} collective-permute-done((bf16[3,128,128]{2,1,0:T(8,128)(2,1)S(1)}, bf16[3,128,128]{2,1,0:T(8,128)(2,1)S(1)}, u32[]{:S(2)}, u32[]{:S(2)}) %collective-permute-start.8) | collective-permute-done | bytes 98336 | tf_op jit(solution)/shard_map/ppermute | solution.py:266
  33.5 0.1 collective-permute-start.12
  33.6 3.2 %collective-permute-start.14 = (bf16[3,128,128]{2,1,0:T(8,128)(2,1)S(1)}, bf16[3,128,128]{2,1,0:T(8,128)(2,1)S(1)}, u32[]{:S(2)}, u32[]{:S(2)}) collective-permute-start(bf16[3,128,128]{2,1,0:T(8,128)(2,1)S(1)} %get-tuple-element.60), channel_id=1, source_target_pairs={{0,30},{1,27},{2,28},{3,25},{4,26},{5,31},{6,24},{7,29},{8,22},{9,... | collective-permute-start | bytes 294920 | tf_op jit(solution)/shard_map/ppermute | solution.py:266
  36.7 0.9 %collective-permute-start.13 = (bf16[3,128,128]{2,1,0:T(8,128)(2,1)S(1)}, bf16[3,128,128]{2,1,0:T(8,128)(2,1)S(1)}, u32[]{:S(2)}, u32[]{:S(2)}) collective-permute-start(bf16[3,128,128]{2,1,0:T(8,128)(2,1)S(1)} %get-tuple-element.58), channel_id=1, source_target_pairs={{0,2},{1,9},{2,0},{3,11},{4,6},{5,13},{6,4},{7,15},{8,10},{9,1},{1... | collective-permute-start | bytes 294920 | tf_op jit(solution)/shard_map/ppermute | solution.py:266
  37.6 5.7 %collective-permute-done.12.rest_13_ = bf16[3,128,128]{2,1,0:T(8,128)(2,1)S(1)} collective-permute-done((bf16[3,128,128]{2,1,0:T(8,128)(2,1)S(1)}, bf16[3,128,128]{2,1,0:T(8,128)(2,1)S(1)}, u32[]{:S(2)}, u32[]{:S(2)}) %collective-permute-start.12) | collective-permute-done | bytes 98336 | tf_op jit(solution)/shard_map/ppermute | solution.py:266
  43.3 2.4 %fit_and_gram.1 = s16[16,80,128]{2,1,0:T(8,128)(2,1)} custom-call(bf16[256,256]{1,0:T(8,128)(2,1)S(1)} %get-tuple-element.34.mixer, bf16[3,128,128]{2,1,0:T(8,128)(2,1)S(1)} %get-tuple-element.35.rest_0_, bf16[3,128,128]{2,1,0:T(8,128)(2,1)S(1)} %collective-permute-done.rest_1_, bf16[3,128,128]{2,1,0:T(8,128)(2,1)S(1)} %collective-permute-done.1.rest_2_, ...), custom_call_target="tpu_custom_call" | custom-call | tf_op jit(solution)/shard_map/fit_and_gram/pallas_call | solution.py:268
  45.7 4.5 %all-to-all-start = ((s16[16,80,128]{2,1,0:T(8,128)(2,1)}), s16[16,80,128]{2,1,0:T(8,128)(2,1)S(1)}, u32[]{:S(2)}, u32[]{:S(2)}) async-start(s16[16,80,128]{2,1,0:T(8,128)(2,1)} %fit_and_gram.1), calls=%async_computation | async-start | bytes 655360 | tf_op jit(solution)/shard_map/all_to_all | solution.py:279
  50.2 9.0 %all-to-all-done.received = s16[16,80,128]{2,1,0:T(8,128)(2,1)S(1)} async-done(((s16[16,80,128]{2,1,0:T(8,128)(2,1)}), s16[16,80,128]{2,1,0:T(8,128)(2,1)S(1)}, u32[]{:S(2)}, u32[]{:S(2)}) %all-to-all-start) | async-done | bytes 327712 | tf_op jit(solution)/shard_map/all_to_all | solution.py:279
  59.2 0.3 band_sum.1.part
  59.5 0.9 %collective-permute-done.15.rim = s16[1,80,128]{2,1,0:T(8,128)(2,1)S(1)} collective-permute-done((s16[1,80,128]{2,1,0:T(8,128)(2,1)S(1)}, s16[1,80,128]{2,1,0:T(8,128)(2,1)S(1)}, u32[]{:S(2)}, u32[]{:S(2)}) %collective-permute-start.15) | collective-permute-done | bytes 20512 | tf_op jit(solution)/shard_map/ppermute | solution.py:282
  60.4 0.8 %band_rim.1 = f32[5,16,1024]{2,1,0:T(8,128)} custom-call(f32[5,16,1024]{2,1,0:T(8,128)S(1)} %band_sum.1.part, s16[1,80,128]{2,1,0:T(8,128)(2,1)S(1)} %collective-permute-done.15.rim), custom_call_target="tpu_custom_call" | custom-call | tf_op jit(solution)/shard_map/band_rim/pallas_call | solution.py:292
  (10 shorter events, 0.0 us)
Async XLA Ops:
  0.0 18.0 %copy-start = (bf16[16,16]{1,0:T(8,128)(2,1)S(1)}, bf16[16,16]{1,0:T(8,128)(2,1)}, u32[]{:S(2)}) copy-start(bf16[16,16]{1,0:T(8,128)(2,1)} %rest_0_.1) | copy-start | bytes 1540
  1.8 9.8 %collective-permute-start = (bf16[3,128,128]{2,1,0:T(8,128)(2,1)S(1)}, bf16[3,128,128]{2,1,0:T(8,128)(2,1)S(1)}, u32[]{:S(2)}, u32[]{:S(2)}) collective-permute-start(bf16[3,128,128]{2,1,0:T(8,128)(2,1)S(1)} %get-tuple-element.33.rest_1_), channel_id=1, source_target_pairs={{0,16},{1,21},{2,18},{3,23},{4,20},{5,17},{6,22},{7,19},{8,24},{9,... | collective-permute-start | bytes 294920 | tf_op jit(solution)/shard_map/ppermute | solution.py:266
  5.9 8.7 %collective-permute-start.2 = (bf16[3,128,128]{2,1,0:T(8,128)(2,1)S(1)}, bf16[3,128,128]{2,1,0:T(8,128)(2,1)S(1)}, u32[]{:S(2)}, u32[]{:S(2)}) collective-permute-start(bf16[3,128,128]{2,1,0:T(8,128)(2,1)S(1)} %get-tuple-element.37), channel_id=1, source_target_pairs={{0,14},{1,23},{2,12},{3,21},{4,10},{5,19},{6,8},{7,17},{8,6},{9,31... | collective-permute-start | bytes 294920 | tf_op jit(solution)/shard_map/ppermute | solution.py:266
  9.3 7.9 %collective-permute-start.1 = (bf16[3,128,128]{2,1,0:T(8,128)(2,1)S(1)}, bf16[3,128,128]{2,1,0:T(8,128)(2,1)S(1)}, u32[]{:S(2)}, u32[]{:S(2)}) collective-permute-start(bf16[3,128,128]{2,1,0:T(8,128)(2,1)S(1)} %get-tuple-element.36), channel_id=1, source_target_pairs={{0,26},{1,11},{2,24},{3,9},{4,30},{5,15},{6,28},{7,13},{8,18},{9,3... | collective-permute-start | bytes 294920 | tf_op jit(solution)/shard_map/ppermute | solution.py:266
  9.5 10.6 %collective-permute-start.3 = (bf16[3,128,128]{2,1,0:T(8,128)(2,1)S(1)}, bf16[3,128,128]{2,1,0:T(8,128)(2,1)S(1)}, u32[]{:S(2)}, u32[]{:S(2)}) collective-permute-start(bf16[3,128,128]{2,1,0:T(8,128)(2,1)S(1)} %get-tuple-element.38), channel_id=1, source_target_pairs={{0,12},{1,15},{2,14},{3,13},{4,8},{5,11},{6,10},{7,9},{8,4},{9,7},... | collective-permute-start | bytes 294920 | tf_op jit(solution)/shard_map/ppermute | solution.py:266
  11.6 12.0 %collective-permute-start.4 = (bf16[3,128,128]{2,1,0:T(8,128)(2,1)S(1)}, bf16[3,128,128]{2,1,0:T(8,128)(2,1)S(1)}, u32[]{:S(2)}, u32[]{:S(2)}) collective-permute-start(bf16[3,128,128]{2,1,0:T(8,128)(2,1)S(1)} %get-tuple-element.40), channel_id=1, source_target_pairs={{0,18},{1,31},{2,16},{3,29},{4,22},{5,27},{6,20},{7,25},{8,26},{9,... | collective-permute-start | bytes 294920 | tf_op jit(solution)/shard_map/ppermute | solution.py:266
  14.6 10.1 %collective-permute-start.6 = (bf16[3,128,128]{2,1,0:T(8,128)(2,1)S(1)}, bf16[3,128,128]{2,1,0:T(8,128)(2,1)S(1)}, u32[]{:S(2)}, u32[]{:S(2)}) collective-permute-start(bf16[3,128,128]{2,1,0:T(8,128)(2,1)S(1)} %get-tuple-element.44), channel_id=1, source_target_pairs={{0,24},{1,17},{2,26},{3,19},{4,28},{5,21},{6,30},{7,23},{8,16},{9,... | collective-permute-start | bytes 294920 | tf_op jit(solution)/shard_map/ppermute | solution.py:266
  17.3 8.4 %collective-permute-start.5 = (bf16[3,128,128]{2,1,0:T(8,128)(2,1)S(1)}, bf16[3,128,128]{2,1,0:T(8,128)(2,1)S(1)}, u32[]{:S(2)}, u32[]{:S(2)}) collective-permute-start(bf16[3,128,128]{2,1,0:T(8,128)(2,1)S(1)} %get-tuple-element.42), channel_id=1, source_target_pairs={{0,10},{1,13},{2,8},{3,15},{4,14},{5,9},{6,12},{7,11},{8,2},{9,5},... | collective-permute-start | bytes 294920 | tf_op jit(solution)/shard_map/ppermute | solution.py:266
  20.2 7.3 %collective-permute-start.7 = (bf16[3,128,128]{2,1,0:T(8,128)(2,1)S(1)}, bf16[3,128,128]{2,1,0:T(8,128)(2,1)S(1)}, u32[]{:S(2)}, u32[]{:S(2)}) collective-permute-start(bf16[3,128,128]{2,1,0:T(8,128)(2,1)S(1)} %get-tuple-element.46), channel_id=1, source_target_pairs={{0,8},{1,29},{2,10},{3,31},{4,12},{5,25},{6,14},{7,27},{8,0},{9,21... | collective-permute-start | bytes 294920 | tf_op jit(solution)/shard_map/ppermute | solution.py:266
  23.6 9.9 %collective-permute-start.8 = (bf16[3,128,128]{2,1,0:T(8,128)(2,1)S(1)}, bf16[3,128,128]{2,1,0:T(8,128)(2,1)S(1)}, u32[]{:S(2)}, u32[]{:S(2)}) collective-permute-start(bf16[3,128,128]{2,1,0:T(8,128)(2,1)S(1)} %get-tuple-element.48), channel_id=1, source_target_pairs={{0,20},{1,25},{2,22},{3,27},{4,16},{5,29},{6,18},{7,31},{8,28},{9,... | collective-permute-start | bytes 294920 | tf_op jit(solution)/shard_map/ppermute | solution.py:266
  24.7 8.9 %collective-permute-start.10 = (bf16[3,128,128]{2,1,0:T(8,128)(2,1)S(1)}, bf16[3,128,128]{2,1,0:T(8,128)(2,1)S(1)}, u32[]{:S(2)}, u32[]{:S(2)}) collective-permute-start(bf16[3,128,128]{2,1,0:T(8,128)(2,1)S(1)} %get-tuple-element.52), channel_id=1, source_target_pairs={{0,4},{1,7},{2,6},{3,5},{4,0},{5,3},{6,2},{7,1},{8,12},{9,15},{10,... | collective-permute-start | bytes 294920 | tf_op jit(solution)/shard_map/ppermute | solution.py:266
  25.6 11.1 %collective-permute-start.9 = (bf16[3,128,128]{2,1,0:T(8,128)(2,1)S(1)}, bf16[3,128,128]{2,1,0:T(8,128)(2,1)S(1)}, u32[]{:S(2)}, u32[]{:S(2)}) collective-permute-start(bf16[3,128,128]{2,1,0:T(8,128)(2,1)S(1)} %get-tuple-element.50), channel_id=1, source_target_pairs={{0,6},{1,3},{2,4},{3,1},{4,2},{5,7},{6,0},{7,5},{8,14},{9,11},{10,... | collective-permute-start | bytes 294920 | tf_op jit(solution)/shard_map/ppermute | solution.py:266
  27.5 10.2 %collective-permute-start.11 = (bf16[3,128,128]{2,1,0:T(8,128)(2,1)S(1)}, bf16[3,128,128]{2,1,0:T(8,128)(2,1)S(1)}, u32[]{:S(2)}, u32[]{:S(2)}) collective-permute-start(bf16[3,128,128]{2,1,0:T(8,128)(2,1)S(1)} %get-tuple-element.54), channel_id=1, source_target_pairs={{0,28},{1,19},{2,30},{3,17},{4,24},{5,23},{6,26},{7,21},{8,20},{9,... | collective-permute-start | bytes 294920 | tf_op jit(solution)/shard_map/ppermute | solution.py:266
  33.5 9.9 %collective-permute-start.12 = (bf16[3,128,128]{2,1,0:T(8,128)(2,1)S(1)}, bf16[3,128,128]{2,1,0:T(8,128)(2,1)S(1)}, u32[]{:S(2)}, u32[]{:S(2)}) collective-permute-start(bf16[3,128,128]{2,1,0:T(8,128)(2,1)S(1)} %get-tuple-element.56), channel_id=1, source_target_pairs={{0,22},{1,5},{2,20},{3,7},{4,18},{5,1},{6,16},{7,3},{8,30},{9,13},... | collective-permute-start | bytes 294920 | tf_op jit(solution)/shard_map/ppermute | solution.py:266
  33.6 9.8 %collective-permute-start.14 = (bf16[3,128,128]{2,1,0:T(8,128)(2,1)S(1)}, bf16[3,128,128]{2,1,0:T(8,128)(2,1)S(1)}, u32[]{:S(2)}, u32[]{:S(2)}) collective-permute-start(bf16[3,128,128]{2,1,0:T(8,128)(2,1)S(1)} %get-tuple-element.60), channel_id=1, source_target_pairs={{0,30},{1,27},{2,28},{3,25},{4,26},{5,31},{6,24},{7,29},{8,22},{9,... | collective-permute-start | bytes 294920 | tf_op jit(solution)/shard_map/ppermute | solution.py:266
  36.7 6.6 %collective-permute-start.13 = (bf16[3,128,128]{2,1,0:T(8,128)(2,1)S(1)}, bf16[3,128,128]{2,1,0:T(8,128)(2,1)S(1)}, u32[]{:S(2)}, u32[]{:S(2)}) collective-permute-start(bf16[3,128,128]{2,1,0:T(8,128)(2,1)S(1)} %get-tuple-element.58), channel_id=1, source_target_pairs={{0,2},{1,9},{2,0},{3,11},{4,6},{5,13},{6,4},{7,15},{8,10},{9,1},{1... | collective-permute-start | bytes 294920 | tf_op jit(solution)/shard_map/ppermute | solution.py:266
  45.7 13.5 %all-to-all-start = ((s16[16,80,128]{2,1,0:T(8,128)(2,1)}), s16[16,80,128]{2,1,0:T(8,128)(2,1)S(1)}, u32[]{:S(2)}, u32[]{:S(2)}) async-start(s16[16,80,128]{2,1,0:T(8,128)(2,1)} %fit_and_gram.1), calls=%async_computation | async-start | bytes 655360 | tf_op jit(solution)/shard_map/all_to_all | solution.py:279
  59.2 1.2 %collective-permute-start.15 = (s16[1,80,128]{2,1,0:T(8,128)(2,1)S(1)}, s16[1,80,128]{2,1,0:T(8,128)(2,1)S(1)}, u32[]{:S(2)}, u32[]{:S(2)}) collective-permute-start(s16[1,80,128]{2,1,0:T(8,128)(2,1)S(1)} %constant_dynamic-slice_fusion), channel_id=1, source_target_pairs={{0,1},{1,0},{2,3},{3,2},{4,5},{5,4},{6,7},{7,6},{8,9},{9,8},{10,11... | collective-permute-start | bytes 61448 | tf_op jit(solution)/shard_map/ppermute | solution.py:282

commit v5 on v4

--- a/solution.py
+++ b/solution.py
@@ -15,6 +15,7 @@
     [8, 13, 7, 6, 9, 5, 12, 4, 10, 3, 2, 14, 11, 1, 15],
     [10, 5, 11, 7, 15, 6, 8, 14, 12, 1, 3, 9, 2, 4, 13],
 )
+CENTRAL = [4, 12, 8, 0, 5, 13, 9, 1, 6, 14, 10, 2, 7, 15, 11, 3]
 WINDOWS = [4] * 15
 PARTS = 2
 STEPS = 128.0
@@ -29,6 +30,12 @@
     for k in range(1, half):
         order += [k, half + k]
     return order, order
+
+
+def transpose_order(devices):
+    if devices == len(CENTRAL):
+        return CENTRAL
+    return list(range(devices // 2, devices)) + list(range(devices // 2))
 
 
 def partner(t):
@@ -136,7 +143,7 @@
     lane = lax.broadcasted_iota(jnp.int32, (ROWS, tile), 1)
     owners = coded.shape[0]
     per = tile // owners
-    for a in range(owners):
+    for slot, a in enumerate(transpose_order(owners)):
         codes, scales = [], jnp.zeros((ROWS, tile), jnp.float32)
         for d in range(reach):
             rows = gram[d * tile + a * per : d * tile + (a + 1) * per]
@@ -146,7 +153,7 @@
             codes += [code[:, d2 * tile : (d2 + 1) * tile] for d2 in range(reach)]
             scales = jnp.where(lane == d, scale, scales)
         sent = jnp.concatenate(codes + [scales], axis=0)
-        coded[a] = sent.astype(jnp.int32).astype(jnp.int16)
+        coded[slot] = sent.astype(jnp.int32).astype(jnp.int16)
 
 
 def encode(rows):
@@ -179,8 +186,9 @@
             for r in range(per):
                 band[e, m : m + 1, r * tile : (r + 1) * tile] = total[r : r + 1]
 
+    order = transpose_order(centres)
     for c in range(centres):
-        blocks = decode(received[c], reach)
+        blocks = decode(received[order.index(c)], reach)
         for d in range(reach):
             m = c + d - middle
             if 0 <= m < centres:
@@ -276,8 +284,11 @@
         compiler_params=FAST,
         name="fit_and_gram",
     )(mixer, *pieces)
-    received = lax.all_to_all(coded, "aux", split_axis=0, concat_axis=0, tiled=True)
-    edge = jnp.where(lax.axis_index("bas") == 0, tiles - 1, 0)
+    order = transpose_order(aux)
+    received = lax.all_to_all(
+        coded, "aux", split_axis=0, concat_axis=0, tiled=True, axis_index_groups=[order]
+    )
+    edge = jnp.where(lax.axis_index("bas") == 0, order.index(tiles - 1), order.index(0))
     edge_tile = lax.dynamic_slice_in_dim(received, edge, 1, 0)
     rim = lax.ppermute(edge_tile, "bas", [(0, 1), (1, 0)])
     share = jax.ShapeDtypeStruct((2 * reach - 1, tiles, tile * tile // aux), jnp.float32)

time: 61.4 us -> 59.7 us (0.972)
  waiting for transfers between devices: 21.4 us -> 19.3 us
    all_to_all x1, waiting for transfers between devices: 9 us -> 6.83 us  [body(): lax.all_to_all(coded, 'aux', split_axis=0, concat_axis=0, tiled=True, axi...]
where the time goes in v5:
time: 59.7 us; the launch traced here: 59.5 us
  starting transfers between devices  32.7 us (55%)
  waiting for transfers between devices  19.3 us (32%)
  Pallas kernels  7.39 us (12%)
    ppermute x15, starting transfers between devices, body(): moved.append(lax.ppermute(piece, ('aux', 'bas'), pairs))  27.8 us
    ppermute x15, waiting for transfers between devices, body(): moved.append(lax.ppermute(piece, ('aux', 'bas'), pairs))  11.5 us
    all_to_all x1, waiting for transfers between devices, body(): lax.all_to_all(coded, 'aux', split_axis=0, concat_axis=0, tiled=True, axi...  6.83 us
    all_to_all x1, starting transfers between devices, body(): lax.all_to_all(coded, 'aux', split_axis=0, concat_axis=0, tiled=True, axi...  4.94 us
    pallas_call x2, Pallas kernels, half_rows(): pl.pallas_call(functools.partial(half_kernel, slots), out_shape=[jax.Shap...  3.93 us
    pallas_call x1, Pallas kernels, body(): pl.pallas_call(gram_kernel, out_shape=jax.ShapeDtypeStruct((aux, (reach *...  2.37 us
  transfers between devices with their start and end apart: 17, of which 8 were waited for; matrix products, arithmetic and copies ran while one was open for 0% of the time, Pallas kernels for 4%

profile of v5, /device:TPU:0, one launch (start us, length us, event | category | flops | bytes accessed | tf_op | source)
XLA Modules:
  0.0 59.5 jit_solution(12577532045384072302)
XLA Ops:
  0.0 1.8 %half_early.1 = (bf16[3,128,128]{2,1,0:T(8,128)(2,1)S(1)}, bf16[3,128,128]{2,1,0:T(8,128)(2,1)S(1)}, bf16[3,128,128]{2,1,0:T(8,128)(2,1)S(1)}, bf16[3,128,128]{2...) custom-call(s32[16]{0:T(128)} %locality.3, ...), custom_call_target="tpu_custom_call" | custom-call | tf_op jit(solution)/shard_map/half_early/pallas_call | solution.py:239
  1.8 4.1 %collective-permute-start = (bf16[3,128,128]{2,1,0:T(8,128)(2,1)S(1)}, bf16[3,128,128]{2,1,0:T(8,128)(2,1)S(1)}, u32[]{:S(2)}, u32[]{:S(2)}) collective-permute-start(bf16[3,128,128]{2,1,0:T(8,128)(2,1)S(1)} %get-tuple-element.33.rest_1_), channel_id=1, source_target_pairs={{0,16},{1,21},{2,18},{3,23},{4,20},{5,17},{6,22},{7,19},{8,24},{9,... | collective-permute-start | bytes 294920 | tf_op jit(solution)/shard_map/ppermute | solution.py:274
  5.9 3.5 %collective-permute-start.2 = (bf16[3,128,128]{2,1,0:T(8,128)(2,1)S(1)}, bf16[3,128,128]{2,1,0:T(8,128)(2,1)S(1)}, u32[]{:S(2)}, u32[]{:S(2)}) collective-permute-start(bf16[3,128,128]{2,1,0:T(8,128)(2,1)S(1)} %get-tuple-element.37), channel_id=1, source_target_pairs={{0,14},{1,23},{2,12},{3,21},{4,10},{5,19},{6,8},{7,17},{8,6},{9,31... | collective-permute-start | bytes 294920 | tf_op jit(solution)/shard_map/ppermute | solution.py:274
  9.3 0.2 collective-permute-start.1
  9.5 0.6 %collective-permute-start.3 = (bf16[3,128,128]{2,1,0:T(8,128)(2,1)S(1)}, bf16[3,128,128]{2,1,0:T(8,128)(2,1)S(1)}, u32[]{:S(2)}, u32[]{:S(2)}) collective-permute-start(bf16[3,128,128]{2,1,0:T(8,128)(2,1)S(1)} %get-tuple-element.38), channel_id=1, source_target_pairs={{0,12},{1,15},{2,14},{3,13},{4,8},{5,11},{6,10},{7,9},{8,4},{9,7},... | collective-permute-start | bytes 294920 | tf_op jit(solution)/shard_map/ppermute | solution.py:274
  10.2 1.4 %collective-permute-done.rest_1_ = bf16[3,128,128]{2,1,0:T(8,128)(2,1)S(1)} collective-permute-done((bf16[3,128,128]{2,1,0:T(8,128)(2,1)S(1)}, bf16[3,128,128]{2,1,0:T(8,128)(2,1)S(1)}, u32[]{:S(2)}, u32[]{:S(2)}) %collective-permute-start) | collective-permute-done | bytes 98336 | tf_op jit(solution)/shard_map/ppermute | solution.py:274
  11.6 3.0 %collective-permute-start.4 = (bf16[3,128,128]{2,1,0:T(8,128)(2,1)S(1)}, bf16[3,128,128]{2,1,0:T(8,128)(2,1)S(1)}, u32[]{:S(2)}, u32[]{:S(2)}) collective-permute-start(bf16[3,128,128]{2,1,0:T(8,128)(2,1)S(1)} %get-tuple-element.40), channel_id=1, source_target_pairs={{0,18},{1,31},{2,16},{3,29},{4,22},{5,27},{6,20},{7,25},{8,26},{9,... | collective-permute-start | bytes 294920 | tf_op jit(solution)/shard_map/ppermute | solution.py:274
  14.6 0.0 collective-permute-done.2.rest_3_
  14.6 2.5 %collective-permute-start.6 = (bf16[3,128,128]{2,1,0:T(8,128)(2,1)S(1)}, bf16[3,128,128]{2,1,0:T(8,128)(2,1)S(1)}, u32[]{:S(2)}, u32[]{:S(2)}) collective-permute-start(bf16[3,128,128]{2,1,0:T(8,128)(2,1)S(1)} %get-tuple-element.44), channel_id=1, source_target_pairs={{0,24},{1,17},{2,26},{3,19},{4,28},{5,21},{6,30},{7,23},{8,16},{9,... | collective-permute-start | bytes 294920 | tf_op jit(solution)/shard_map/ppermute | solution.py:274
  17.1 0.2 collective-permute-done.1.rest_2_
  17.3 0.7 %collective-permute-start.5 = (bf16[3,128,128]{2,1,0:T(8,128)(2,1)S(1)}, bf16[3,128,128]{2,1,0:T(8,128)(2,1)S(1)}, u32[]{:S(2)}, u32[]{:S(2)}) collective-permute-start(bf16[3,128,128]{2,1,0:T(8,128)(2,1)S(1)} %get-tuple-element.42), channel_id=1, source_target_pairs={{0,10},{1,13},{2,8},{3,15},{4,14},{5,9},{6,12},{7,11},{8,2},{9,5},... | collective-permute-start | bytes 294920 | tf_op jit(solution)/shard_map/ppermute | solution.py:274
  18.0 2.2 %half_late.1 = (bf16[3,128,128]{2,1,0:T(8,128)(2,1)S(1)}, bf16[3,128,128]{2,1,0:T(8,128)(2,1)S(1)}, bf16[3,128,128]{2,1,0:T(8,128)(2,1)S(1)}, bf16[3,128,128]{2,...) custom-call(s32[16]{0:T(128)} %locality.3, ...), custom_call_target="tpu_custom_call" | custom-call | tf_op jit(solution)/shard_map/half_late/pallas_call | solution.py:239
  20.2 1.9 %collective-permute-start.7 = (bf16[3,128,128]{2,1,0:T(8,128)(2,1)S(1)}, bf16[3,128,128]{2,1,0:T(8,128)(2,1)S(1)}, u32[]{:S(2)}, u32[]{:S(2)}) collective-permute-start(bf16[3,128,128]{2,1,0:T(8,128)(2,1)S(1)} %get-tuple-element.46), channel_id=1, source_target_pairs={{0,8},{1,29},{2,10},{3,31},{4,12},{5,25},{6,14},{7,27},{8,0},{9,21... | collective-permute-start | bytes 294920 | tf_op jit(solution)/shard_map/ppermute | solution.py:274
  22.0 1.5 %collective-permute-done.4.rest_5_ = bf16[3,128,128]{2,1,0:T(8,128)(2,1)S(1)} collective-permute-done((bf16[3,128,128]{2,1,0:T(8,128)(2,1)S(1)}, bf16[3,128,128]{2,1,0:T(8,128)(2,1)S(1)}, u32[]{:S(2)}, u32[]{:S(2)}) %collective-permute-start.4) | collective-permute-done | bytes 98336 | tf_op jit(solution)/shard_map/ppermute | solution.py:274
  23.6 1.1 %collective-permute-start.8 = (bf16[3,128,128]{2,1,0:T(8,128)(2,1)S(1)}, bf16[3,128,128]{2,1,0:T(8,128)(2,1)S(1)}, u32[]{:S(2)}, u32[]{:S(2)}) collective-permute-start(bf16[3,128,128]{2,1,0:T(8,128)(2,1)S(1)} %get-tuple-element.48), channel_id=1, source_target_pairs={{0,20},{1,25},{2,22},{3,27},{4,16},{5,29},{6,18},{7,31},{8,28},{9,... | collective-permute-start | bytes 294920 | tf_op jit(solution)/shard_map/ppermute | solution.py:274
  24.7 0.0 collective-permute-done.6.rest_7_
  24.7 0.8 %collective-permute-start.10 = (bf16[3,128,128]{2,1,0:T(8,128)(2,1)S(1)}, bf16[3,128,128]{2,1,0:T(8,128)(2,1)S(1)}, u32[]{:S(2)}, u32[]{:S(2)}) collective-permute-start(bf16[3,128,128]{2,1,0:T(8,128)(2,1)S(1)} %get-tuple-element.52), channel_id=1, source_target_pairs={{0,4},{1,7},{2,6},{3,5},{4,0},{5,3},{6,2},{7,1},{8,12},{9,15},{10,... | collective-permute-start | bytes 294920 | tf_op jit(solution)/shard_map/ppermute | solution.py:274
  25.5 0.2 collective-permute-done.5.rest_6_
  25.6 1.8 %collective-permute-start.9 = (bf16[3,128,128]{2,1,0:T(8,128)(2,1)S(1)}, bf16[3,128,128]{2,1,0:T(8,128)(2,1)S(1)}, u32[]{:S(2)}, u32[]{:S(2)}) collective-permute-start(bf16[3,128,128]{2,1,0:T(8,128)(2,1)S(1)} %get-tuple-element.50), channel_id=1, source_target_pairs={{0,6},{1,3},{2,4},{3,1},{4,2},{5,7},{6,0},{7,5},{8,14},{9,11},{10,... | collective-permute-start | bytes 294920 | tf_op jit(solution)/shard_map/ppermute | solution.py:274
  27.4 0.0 collective-permute-done.7.rest_8_
  27.5 3.5 %collective-permute-start.11 = (bf16[3,128,128]{2,1,0:T(8,128)(2,1)S(1)}, bf16[3,128,128]{2,1,0:T(8,128)(2,1)S(1)}, u32[]{:S(2)}, u32[]{:S(2)}) collective-permute-start(bf16[3,128,128]{2,1,0:T(8,128)(2,1)S(1)} %get-tuple-element.54), channel_id=1, source_target_pairs={{0,28},{1,19},{2,30},{3,17},{4,24},{5,23},{6,26},{7,21},{8,20},{9,... | collective-permute-start | bytes 294920 | tf_op jit(solution)/shard_map/ppermute | solution.py:274
  30.9 2.5 %collective-permute-done.8.rest_9_ = bf16[3,128,128]{2,1,0:T(8,128)(2,1)S(1)} collective-permute-done((bf16[3,128,128]{2,1,0:T(8,128)(2,1)S(1)}, bf16[3,128,128]{2,1,0:T(8,128)(2,1)S(1)}, u32[]{:S(2)}, u32[]{:S(2)}) %collective-permute-start.8) | collective-permute-done | bytes 98336 | tf_op jit(solution)/shard_map/ppermute | solution.py:274
  33.5 0.1 collective-permute-start.12
  33.6 3.2 %collective-permute-start.14 = (bf16[3,128,128]{2,1,0:T(8,128)(2,1)S(1)}, bf16[3,128,128]{2,1,0:T(8,128)(2,1)S(1)}, u32[]{:S(2)}, u32[]{:S(2)}) collective-permute-start(bf16[3,128,128]{2,1,0:T(8,128)(2,1)S(1)} %get-tuple-element.60), channel_id=1, source_target_pairs={{0,30},{1,27},{2,28},{3,25},{4,26},{5,31},{6,24},{7,29},{8,22},{9,... | collective-permute-start | bytes 294920 | tf_op jit(solution)/shard_map/ppermute | solution.py:274
  36.7 0.9 %collective-permute-start.13 = (bf16[3,128,128]{2,1,0:T(8,128)(2,1)S(1)}, bf16[3,128,128]{2,1,0:T(8,128)(2,1)S(1)}, u32[]{:S(2)}, u32[]{:S(2)}) collective-permute-start(bf16[3,128,128]{2,1,0:T(8,128)(2,1)S(1)} %get-tuple-element.58), channel_id=1, source_target_pairs={{0,2},{1,9},{2,0},{3,11},{4,6},{5,13},{6,4},{7,15},{8,10},{9,1},{1... | collective-permute-start | bytes 294920 | tf_op jit(solution)/shard_map/ppermute | solution.py:274
  37.6 5.7 %collective-permute-done.12.rest_13_ = bf16[3,128,128]{2,1,0:T(8,128)(2,1)S(1)} collective-permute-done((bf16[3,128,128]{2,1,0:T(8,128)(2,1)S(1)}, bf16[3,128,128]{2,1,0:T(8,128)(2,1)S(1)}, u32[]{:S(2)}, u32[]{:S(2)}) %collective-permute-start.12) | collective-permute-done | bytes 98336 | tf_op jit(solution)/shard_map/ppermute | solution.py:274
  43.3 2.4 %fit_and_gram.1 = s16[16,80,128]{2,1,0:T(8,128)(2,1)} custom-call(bf16[256,256]{1,0:T(8,128)(2,1)S(1)} %get-tuple-element.34.mixer, bf16[3,128,128]{2,1,0:T(8,128)(2,1)S(1)} %get-tuple-element.35.rest_0_, bf16[3,128,128]{2,1,0:T(8,128)(2,1)S(1)} %collective-permute-done.rest_1_, bf16[3,128,128]{2,1,0:T(8,128)(2,1)S(1)} %collective-permute-done.1.rest_2_, ...), custom_call_target="tpu_custom_call" | custom-call | tf_op jit(solution)/shard_map/fit_and_gram/pallas_call | solution.py:276
  45.7 4.9 %all-to-all-start = ((s16[16,80,128]{2,1,0:T(8,128)(2,1)}), s16[16,80,128]{2,1,0:T(8,128)(2,1)S(1)}, u32[]{:S(2)}, u32[]{:S(2)}) async-start(s16[16,80,128]{2,1,0:T(8,128)(2,1)} %fit_and_gram.1), calls=%async_computation | async-start | bytes 655360 | tf_op jit(solution)/shard_map/all_to_all | solution.py:288
  50.6 6.8 %all-to-all-done.received = s16[16,80,128]{2,1,0:T(8,128)(2,1)S(1)} async-done(((s16[16,80,128]{2,1,0:T(8,128)(2,1)}), s16[16,80,128]{2,1,0:T(8,128)(2,1)S(1)}, u32[]{:S(2)}, u32[]{:S(2)}) %all-to-all-start) | async-done | bytes 327712 | tf_op jit(solution)/shard_map/all_to_all | solution.py:288
  57.5 0.3 band_sum.1.part
  57.8 0.9 %collective-permute-done.15.rim = s16[1,80,128]{2,1,0:T(8,128)(2,1)S(1)} collective-permute-done((s16[1,80,128]{2,1,0:T(8,128)(2,1)S(1)}, s16[1,80,128]{2,1,0:T(8,128)(2,1)S(1)}, u32[]{:S(2)}, u32[]{:S(2)}) %collective-permute-start.15) | collective-permute-done | bytes 20512 | tf_op jit(solution)/shard_map/ppermute | solution.py:293
  58.7 0.8 %band_rim.1 = f32[5,16,1024]{2,1,0:T(8,128)} custom-call(f32[5,16,1024]{2,1,0:T(8,128)S(1)} %band_sum.1.part, s16[1,80,128]{2,1,0:T(8,128)(2,1)S(1)} %collective-permute-done.15.rim), custom_call_target="tpu_custom_call" | custom-call | tf_op jit(solution)/shard_map/band_rim/pallas_call | solution.py:303
  (10 shorter events, 0.0 us)
Async XLA Ops:
  0.0 18.0 %copy-start = (bf16[16,16]{1,0:T(8,128)(2,1)S(1)}, bf16[16,16]{1,0:T(8,128)(2,1)}, u32[]{:S(2)}) copy-start(bf16[16,16]{1,0:T(8,128)(2,1)} %rest_0_.1) | copy-start | bytes 1540
  1.8 9.8 %collective-permute-start = (bf16[3,128,128]{2,1,0:T(8,128)(2,1)S(1)}, bf16[3,128,128]{2,1,0:T(8,128)(2,1)S(1)}, u32[]{:S(2)}, u32[]{:S(2)}) collective-permute-start(bf16[3,128,128]{2,1,0:T(8,128)(2,1)S(1)} %get-tuple-element.33.rest_1_), channel_id=1, source_target_pairs={{0,16},{1,21},{2,18},{3,23},{4,20},{5,17},{6,22},{7,19},{8,24},{9,... | collective-permute-start | bytes 294920 | tf_op jit(solution)/shard_map/ppermute | solution.py:274
  5.9 8.7 %collective-permute-start.2 = (bf16[3,128,128]{2,1,0:T(8,128)(2,1)S(1)}, bf16[3,128,128]{2,1,0:T(8,128)(2,1)S(1)}, u32[]{:S(2)}, u32[]{:S(2)}) collective-permute-start(bf16[3,128,128]{2,1,0:T(8,128)(2,1)S(1)} %get-tuple-element.37), channel_id=1, source_target_pairs={{0,14},{1,23},{2,12},{3,21},{4,10},{5,19},{6,8},{7,17},{8,6},{9,31... | collective-permute-start | bytes 294920 | tf_op jit(solution)/shard_map/ppermute | solution.py:274
  9.3 7.9 %collective-permute-start.1 = (bf16[3,128,128]{2,1,0:T(8,128)(2,1)S(1)}, bf16[3,128,128]{2,1,0:T(8,128)(2,1)S(1)}, u32[]{:S(2)}, u32[]{:S(2)}) collective-permute-start(bf16[3,128,128]{2,1,0:T(8,128)(2,1)S(1)} %get-tuple-element.36), channel_id=1, source_target_pairs={{0,26},{1,11},{2,24},{3,9},{4,30},{5,15},{6,28},{7,13},{8,18},{9,3... | collective-permute-start | bytes 294920 | tf_op jit(solution)/shard_map/ppermute | solution.py:274
  9.5 10.6 %collective-permute-start.3 = (bf16[3,128,128]{2,1,0:T(8,128)(2,1)S(1)}, bf16[3,128,128]{2,1,0:T(8,128)(2,1)S(1)}, u32[]{:S(2)}, u32[]{:S(2)}) collective-permute-start(bf16[3,128,128]{2,1,0:T(8,128)(2,1)S(1)} %get-tuple-element.38), channel_id=1, source_target_pairs={{0,12},{1,15},{2,14},{3,13},{4,8},{5,11},{6,10},{7,9},{8,4},{9,7},... | collective-permute-start | bytes 294920 | tf_op jit(solution)/shard_map/ppermute | solution.py:274
  11.6 12.0 %collective-permute-start.4 = (bf16[3,128,128]{2,1,0:T(8,128)(2,1)S(1)}, bf16[3,128,128]{2,1,0:T(8,128)(2,1)S(1)}, u32[]{:S(2)}, u32[]{:S(2)}) collective-permute-start(bf16[3,128,128]{2,1,0:T(8,128)(2,1)S(1)} %get-tuple-element.40), channel_id=1, source_target_pairs={{0,18},{1,31},{2,16},{3,29},{4,22},{5,27},{6,20},{7,25},{8,26},{9,... | collective-permute-start | bytes 294920 | tf_op jit(solution)/shard_map/ppermute | solution.py:274
  14.6 10.1 %collective-permute-start.6 = (bf16[3,128,128]{2,1,0:T(8,128)(2,1)S(1)}, bf16[3,128,128]{2,1,0:T(8,128)(2,1)S(1)}, u32[]{:S(2)}, u32[]{:S(2)}) collective-permute-start(bf16[3,128,128]{2,1,0:T(8,128)(2,1)S(1)} %get-tuple-element.44), channel_id=1, source_target_pairs={{0,24},{1,17},{2,26},{3,19},{4,28},{5,21},{6,30},{7,23},{8,16},{9,... | collective-permute-start | bytes 294920 | tf_op jit(solution)/shard_map/ppermute | solution.py:274
  17.3 8.4 %collective-permute-start.5 = (bf16[3,128,128]{2,1,0:T(8,128)(2,1)S(1)}, bf16[3,128,128]{2,1,0:T(8,128)(2,1)S(1)}, u32[]{:S(2)}, u32[]{:S(2)}) collective-permute-start(bf16[3,128,128]{2,1,0:T(8,128)(2,1)S(1)} %get-tuple-element.42), channel_id=1, source_target_pairs={{0,10},{1,13},{2,8},{3,15},{4,14},{5,9},{6,12},{7,11},{8,2},{9,5},... | collective-permute-start | bytes 294920 | tf_op jit(solution)/shard_map/ppermute | solution.py:274
  20.2 7.3 %collective-permute-start.7 = (bf16[3,128,128]{2,1,0:T(8,128)(2,1)S(1)}, bf16[3,128,128]{2,1,0:T(8,128)(2,1)S(1)}, u32[]{:S(2)}, u32[]{:S(2)}) collective-permute-start(bf16[3,128,128]{2,1,0:T(8,128)(2,1)S(1)} %get-tuple-element.46), channel_id=1, source_target_pairs={{0,8},{1,29},{2,10},{3,31},{4,12},{5,25},{6,14},{7,27},{8,0},{9,21... | collective-permute-start | bytes 294920 | tf_op jit(solution)/shard_map/ppermute | solution.py:274
  23.6 9.9 %collective-permute-start.8 = (bf16[3,128,128]{2,1,0:T(8,128)(2,1)S(1)}, bf16[3,128,128]{2,1,0:T(8,128)(2,1)S(1)}, u32[]{:S(2)}, u32[]{:S(2)}) collective-permute-start(bf16[3,128,128]{2,1,0:T(8,128)(2,1)S(1)} %get-tuple-element.48), channel_id=1, source_target_pairs={{0,20},{1,25},{2,22},{3,27},{4,16},{5,29},{6,18},{7,31},{8,28},{9,... | collective-permute-start | bytes 294920 | tf_op jit(solution)/shard_map/ppermute | solution.py:274
  24.7 8.9 %collective-permute-start.10 = (bf16[3,128,128]{2,1,0:T(8,128)(2,1)S(1)}, bf16[3,128,128]{2,1,0:T(8,128)(2,1)S(1)}, u32[]{:S(2)}, u32[]{:S(2)}) collective-permute-start(bf16[3,128,128]{2,1,0:T(8,128)(2,1)S(1)} %get-tuple-element.52), channel_id=1, source_target_pairs={{0,4},{1,7},{2,6},{3,5},{4,0},{5,3},{6,2},{7,1},{8,12},{9,15},{10,... | collective-permute-start | bytes 294920 | tf_op jit(solution)/shard_map/ppermute | solution.py:274
  25.6 11.1 %collective-permute-start.9 = (bf16[3,128,128]{2,1,0:T(8,128)(2,1)S(1)}, bf16[3,128,128]{2,1,0:T(8,128)(2,1)S(1)}, u32[]{:S(2)}, u32[]{:S(2)}) collective-permute-start(bf16[3,128,128]{2,1,0:T(8,128)(2,1)S(1)} %get-tuple-element.50), channel_id=1, source_target_pairs={{0,6},{1,3},{2,4},{3,1},{4,2},{5,7},{6,0},{7,5},{8,14},{9,11},{10,... | collective-permute-start | bytes 294920 | tf_op jit(solution)/shard_map/ppermute | solution.py:274
  27.5 10.2 %collective-permute-start.11 = (bf16[3,128,128]{2,1,0:T(8,128)(2,1)S(1)}, bf16[3,128,128]{2,1,0:T(8,128)(2,1)S(1)}, u32[]{:S(2)}, u32[]{:S(2)}) collective-permute-start(bf16[3,128,128]{2,1,0:T(8,128)(2,1)S(1)} %get-tuple-element.54), channel_id=1, source_target_pairs={{0,28},{1,19},{2,30},{3,17},{4,24},{5,23},{6,26},{7,21},{8,20},{9,... | collective-permute-start | bytes 294920 | tf_op jit(solution)/shard_map/ppermute | solution.py:274
  33.5 9.9 %collective-permute-start.12 = (bf16[3,128,128]{2,1,0:T(8,128)(2,1)S(1)}, bf16[3,128,128]{2,1,0:T(8,128)(2,1)S(1)}, u32[]{:S(2)}, u32[]{:S(2)}) collective-permute-start(bf16[3,128,128]{2,1,0:T(8,128)(2,1)S(1)} %get-tuple-element.56), channel_id=1, source_target_pairs={{0,22},{1,5},{2,20},{3,7},{4,18},{5,1},{6,16},{7,3},{8,30},{9,13},... | collective-permute-start | bytes 294920 | tf_op jit(solution)/shard_map/ppermute | solution.py:274
  33.6 9.8 %collective-permute-start.14 = (bf16[3,128,128]{2,1,0:T(8,128)(2,1)S(1)}, bf16[3,128,128]{2,1,0:T(8,128)(2,1)S(1)}, u32[]{:S(2)}, u32[]{:S(2)}) collective-permute-start(bf16[3,128,128]{2,1,0:T(8,128)(2,1)S(1)} %get-tuple-element.60), channel_id=1, source_target_pairs={{0,30},{1,27},{2,28},{3,25},{4,26},{5,31},{6,24},{7,29},{8,22},{9,... | collective-permute-start | bytes 294920 | tf_op jit(solution)/shard_map/ppermute | solution.py:274
  36.7 6.6 %collective-permute-start.13 = (bf16[3,128,128]{2,1,0:T(8,128)(2,1)S(1)}, bf16[3,128,128]{2,1,0:T(8,128)(2,1)S(1)}, u32[]{:S(2)}, u32[]{:S(2)}) collective-permute-start(bf16[3,128,128]{2,1,0:T(8,128)(2,1)S(1)} %get-tuple-element.58), channel_id=1, source_target_pairs={{0,2},{1,9},{2,0},{3,11},{4,6},{5,13},{6,4},{7,15},{8,10},{9,1},{1... | collective-permute-start | bytes 294920 | tf_op jit(solution)/shard_map/ppermute | solution.py:274
  45.7 11.8 %all-to-all-start = ((s16[16,80,128]{2,1,0:T(8,128)(2,1)}), s16[16,80,128]{2,1,0:T(8,128)(2,1)S(1)}, u32[]{:S(2)}, u32[]{:S(2)}) async-start(s16[16,80,128]{2,1,0:T(8,128)(2,1)} %fit_and_gram.1), calls=%async_computation | async-start | bytes 655360 | tf_op jit(solution)/shard_map/all_to_all | solution.py:288
  57.5 1.2 %collective-permute-start.15 = (s16[1,80,128]{2,1,0:T(8,128)(2,1)S(1)}, s16[1,80,128]{2,1,0:T(8,128)(2,1)S(1)}, u32[]{:S(2)}, u32[]{:S(2)}) collective-permute-start(s16[1,80,128]{2,1,0:T(8,128)(2,1)S(1)} %constant_dynamic-slice_fusion), channel_id=1, source_target_pairs={{0,1},{1,0},{2,3},{3,2},{4,5},{5,4},{6,7},{7,6},{8,9},{9,8},{10,11... | collective-permute-start | bytes 61448 | tf_op jit(solution)/shard_map/ppermute | solution.py:293
